TPU v7x, 256 devices: a whole 4x4x8 slice. The times are simulated.
256 devices in a mesh: dp: 32 (over y, x, core), mp: 8 (over z).
Axes of the slice: x: 4, y: 4, z: 8, core: 2. Of those that a mesh axis runs over, the one named last changes fastest.
Arguments:
- hidden: bfloat16 [192, 128, 4096], P('dp'), may hold values from -6 to 6
- norm_gain: bfloat16 [4096], replicated, may hold values from 0.25 to 1.75
- w_query: bfloat16 [4096, 4096], P('dp', 'mp'), may hold values from -0.09375 to 0.09375
- w_kv: bfloat16 [4096, 2, 1024], P('dp', None, 'mp'), may hold values from -0.09375 to 0.09375
- w_out: bfloat16 [4096, 4096], P('mp', 'dp'), may hold values from -0.09375 to 0.09375
- w_head: float32 [4096], replicated, may hold values from -0.75 to 0.75
- parents: int32 [192, 16], replicated, may hold values from -1 to 191, as said below
- lengths: int32 [192], replicated, may hold values from 64 to 128, as said below
Outputs:
- layer_out: bfloat16 [192, 128, 4096], P('dp', None, 'mp')
- values: float32 [192], P('dp')
Inputs may be any that keep to these rules, and one draw needn't show every extreme that they name: `parents`: row n lists the ancestors of node n, nearest first, then -1 for the levels it lacks; the list of a node is its parent followed by the parent's list. All 6 nodes held by one index of dp have the same list, and the nodes in a list are held by distinct indices of dp, none the node's own. Some node has 16 ancestors. `lengths`: the used token slots of a node segment are its first ones.
All inputs are finite; a program needn't handle non-finite values.
Results may differ from a plain program's by a relative error of at most 0.017.
Values may be sent and summed in bfloat16 or wider, within the bound.
A program may use at most 128 MiB of HBM per device.

v0:
```python
import jax
import jax.numpy as jnp
from jax import lax
from jax.sharding import PartitionSpec as P

HS = 128


def unit_rows(rows):
    floats = rows.astype(jnp.float32)
    meansq = jnp.mean(floats * floats, axis=-1, keepdims=True)
    return floats * lax.rsqrt(meansq + 1e-05)


def on_device(hidden, norm_gain, w_query, w_kv, w_out, w_head, parents, lengths):
    slots, blk, width = hidden.shape
    count = slots * blk
    rows = hidden.reshape(count, width)
    normed = (unit_rows(rows) * norm_gain.astype(jnp.float32)).astype(jnp.bfloat16)
    q_columns = w_query.shape[1]
    kv_columns = w_kv.shape[2]
    q_whole, kv_whole = (
        lax.all_gather(w_query, "dp", axis=0, tiled=True),
        lax.all_gather(w_kv, "dp", axis=0, tiled=True),
    )
    q_proj = jnp.dot(normed, q_whole, preferred_element_type=jnp.float32)
    kv_proj = jnp.einsum("rd,dpc->prc", normed, kv_whole, preferred_element_type=jnp.float32)
    q_proj = q_proj.astype(jnp.bfloat16)
    kv_proj = kv_proj.astype(jnp.bfloat16)
    heads = q_columns // HS
    kv_heads = kv_columns // HS
    sharing = heads // kv_heads
    devices = lax.axis_size("dp")
    me_index = lax.axis_index("dp")
    levels = parents.shape[1]
    firsts = parents.reshape(devices, slots, levels)[:, 0, :]
    holder = jnp.where(firsts >= 0, firsts // slots, -1)
    mine_hit = holder == me_index
    wanted = jnp.sum(jnp.where(mine_hit, firsts % slots, 0), axis=1)
    present = jnp.any(mine_hit, axis=1)
    local_kv = kv_proj.reshape(2, slots, blk, kv_columns)
    outgoing = jnp.take(local_kv, wanted, axis=1) * present[None, :, None, None].astype(
        jnp.bfloat16
    )
    incoming = lax.all_to_all(outgoing, "dp", split_axis=1, concat_axis=1, tiled=True)
    chain = lax.dynamic_index_in_dim(firsts, me_index, 0, keepdims=False)
    safe = jnp.maximum(chain, 0)
    ancestors = jnp.take(incoming, safe // slots, axis=1)
    anc_len = jnp.where(chain >= 0, jnp.take(lengths, safe), 0)
    own_len = lax.dynamic_slice_in_dim(lengths, me_index * slots, slots)
    query = q_proj.reshape(slots, blk, kv_heads, sharing, HS)
    own_keys = local_kv[0].reshape(slots, blk, kv_heads, HS)
    own_vals = local_kv[1].reshape(slots, blk, kv_heads, HS)
    far_keys = ancestors[0].reshape(levels * blk, kv_heads, HS)
    far_vals = ancestors[1].reshape(levels * blk, kv_heads, HS)
    scale = 1.0 / HS**0.5
    token = jnp.arange(blk, dtype=jnp.int32)
    near_scores = (
        jnp.einsum("stkgd,sukd->skgtu", query, own_keys, preferred_element_type=jnp.float32) * scale
    )
    far_scores = (
        jnp.einsum("stkgd,ukd->skgtu", query, far_keys, preferred_element_type=jnp.float32) * scale
    )
    near_mask = (token[None, :] <= token[:, None])[None] & (
        token[None, None, :] < own_len[:, None, None]
    )
    far_mask = (token[None, :] < anc_len[:, None]).reshape(-1)
    near_weights = jnp.where(near_mask[:, None, None], jnp.exp(near_scores), 0.0)
    far_weights = jnp.where(far_mask[None, None, None, None, :], jnp.exp(far_scores), 0.0)
    denom = jnp.sum(near_weights, axis=-1, keepdims=True) + jnp.sum(
        far_weights, axis=-1, keepdims=True
    )
    near_probs = (near_weights / denom).astype(jnp.bfloat16)
    far_probs = (far_weights / denom).astype(jnp.bfloat16)
    attn = jnp.einsum("skgtu,sukd->stkgd", near_probs, own_vals, preferred_element_type=jnp.float32)
    attn = attn + jnp.einsum(
        "skgtu,ukd->stkgd", far_probs, far_vals, preferred_element_type=jnp.float32
    )
    attn = attn.astype(jnp.bfloat16).reshape(count, q_columns)
    partial_value = jnp.dot(
        attn, lax.all_gather(w_out, "dp", axis=1, tiled=True), preferred_element_type=jnp.float32
    )
    share = width // lax.axis_size("mp")
    first_col = lax.axis_index("mp") * share
    total = lax.psum(partial_value.astype(jnp.bfloat16), "mp").astype(jnp.float32)
    layer_full = (rows.astype(jnp.float32) + total).astype(jnp.bfloat16)
    floats = layer_full.astype(jnp.float32)
    sumsq = jnp.sum(floats * floats, axis=-1)
    product = jnp.sum(floats * w_head[None, :], axis=-1)
    layer_mine = lax.dynamic_slice_in_dim(layer_full, first_col, share, 1)
    token_score = (product * lax.rsqrt(sumsq / width + 1e-05)).reshape(slots, blk)
    used = token[None, :] < own_len[:, None]
    node_score = jnp.sum(jnp.where(used, token_score, 0.0), axis=1) / own_len.astype(jnp.float32)
    local_parents = lax.dynamic_slice_in_dim(parents, me_index * slots, slots, 0)
    onehot = (
        local_parents[:, :, None] == jnp.arange(parents.shape[0], dtype=jnp.int32)[None, None, :]
    ).astype(jnp.float32)
    term = jnp.sum(node_score[:, None, None] * onehot, axis=(0, 1))
    backed = lax.psum_scatter(term, "dp", scatter_dimension=0, tiled=True)
    values = node_score + backed
    return (layer_mine.reshape(slots, blk, share), values)


def solution(mesh):
    in_specs = (
        P("dp", None, None),
        P(),
        P("dp", "mp"),
        P("dp", None, "mp"),
        P("mp", "dp"),
        P(),
        P(),
        P(),
    )
    out_specs = (P("dp", None, "mp"), P("dp"))
    return jax.shard_map(
        on_device, mesh=mesh, in_specs=in_specs, out_specs=out_specs, check_vma=False
    )
```

profile of v0, /device:TPU:1, one launch (start us, length us, event | category | flops | bytes accessed | tf_op | source)
XLA Modules:
  0.0 425.1 jit_solution(6590800682018786882)
XLA Ops:
  7.2 0.0 all-gather.4.cloned.1.call-start
  7.2 1.5 copy.76
  8.7 0.0 all-gather.4.cloned.1.call-update
  8.7 0.0 all-gather.6.cloned.1.call-start
  8.8 0.7 all-gather.6.cloned.1.call-update
  9.5 0.8 copy.78
  10.3 0.1 copy.98
  10.4 0.9 convert_element_type.61
  11.4 4.3 %fusion.5 = f32[6,128]{1,0:T(8,128)S(1)} fusion(bf16[6,128,4096]{2,1,0:T(8,128)(2,1)} %param.8), kind=kLoop, calls=%fused_computation.16 | loop fusion | flops 9436416 | bytes 6294528 | tf_op jit(solution)/shard_map/reduce_sum | solution.py:11
  15.6 0.0 copy-done.1
  15.6 5.4 %fusion.7 = bf16[768,4096]{1,0:T(8,128)(2,1)} fusion(bf16[6,128,4096]{2,1,0:T(8,128)(2,1)S(1)} %copy-done.1, f32[4096]{0:T(1024)S(1)} %convert_element_type.61, f32[768]{0:T(1024)S(1)} %rsqrt_bitcast_fusion), kind=kLoop, calls=%fused_computation.18 | loop fusion | flops 12582912 | bytes 12602368 | tf_op jit(solution)/shard_map/convert_element_type | solution.py:19
  21.0 43.3 %all-gather.4.cloned.1.call-done = bf16[4096,2,128]{2,0,1:T(8,128)(2,1)} async-done(((bf16[128,2,128]{2,0,1:T(8,128)(2,1)}), bf16[4096,2,128]{2,0,1:T(8,128)(2,1)}) %all-gather.4.cloned.1.call-update) | async-done | bytes 2097168 | tf_op jit(solution)/shard_map/all_gather | solution.py:24
  64.3 5.2 %fusion.13 = bf16[768,2,128]{2,0,1:T(8,128)(2,1)S(1)} fusion(bf16[4096,2,128]{2,0,1:T(8,128)(2,1)} %all-gather.4.cloned.1.call-done, bf16[768,4096]{1,0:T(8,128)(2,1)} %fusion.7), kind=kOutput, calls=%fused_computation.29 | convolution fusion | flops 1610809344 | bytes 8781824 | tf_op jit(solution)/shard_map/rd,dpc->prc/dot_general | solution.py:27
  69.5 0.0 copy-start
  69.5 1.0 gather_fusion.1
  70.5 1.6 multiply_bitcast_fusion
  72.1 5.1 %all-to-all-start = ((bf16[2,32,128,128]{3,2,0,1:T(8,128)(2,1)}), bf16[2,32,128,128]{3,2,0,1:T(8,128)(2,1)S(1)}, u32[]{:S(2)}, u32[]{:S(2)}) async-start(bf16[2,32,128,128]{3,2,0,1:T(8,128)(2,1)} %multiply_bitcast_fusion), calls=%async_computation | async-start | bytes 4194304 | tf_op jit(solution)/shard_map/all_to_all | solution.py:45
  77.2 0.0 all-gather.8.cloned.1.call-start
  77.2 0.7 all-gather.8.cloned.1.call-update
  77.9 0.2 all-reduce.3.cloned.1.call-start
  78.1 0.2 compare_reduce_fusion
  78.4 0.2 fusion.32
  78.6 0.0 copy-done
  78.6 0.7 gather_fusion
  79.3 0.1 dynamic_slice.13
  79.4 0.1 iota_compare_fusion.3
  79.5 0.4 copy-done.7
  79.9 0.1 fusion.26
  80.0 0.8 broadcast_and_fusion
  80.8 0.8 fusion.42
  81.5 25.3 %all-to-all-done = bf16[2,32,128,128]{3,2,0,1:T(8,128)(2,1)S(1)} async-done(((bf16[2,32,128,128]{3,2,0,1:T(8,128)(2,1)}), bf16[2,32,128,128]{3,2,0,1:T(8,128)(2,1)S(1)}, u32[]{:S(2)}, u32[]{:S(2)}) %all-to-all-start) | async-done | bytes 2097184 | tf_op jit(solution)/shard_map/all_to_all | solution.py:45
  106.8 0.7 gather_fusion.2
  107.6 0.2 select_bitcast_fusion
  107.8 0.1 fusion.41
  107.9 0.0 copy-start.3
  107.9 0.0 copy-start.4
  107.9 23.6 %all-gather.6.cloned.1.call-done = bf16[4096,512]{1,0:T(8,128)(2,1)} async-done(((bf16[128,512]{1,0:T(8,128)(2,1)}), bf16[4096,512]{1,0:T(8,128)(2,1)}) %all-gather.6.cloned.1.call-update) | async-done | bytes 4194320 | tf_op jit(solution)/shard_map/all_gather | solution.py:23
  131.5 7.4 %convolution_convert_fusion.1 = bf16[768,512]{1,0:T(8,128)(2,1)S(1)} fusion(bf16[768,4096]{1,0:T(8,128)(2,1)} %fusion.7, bf16[4096,512]{1,0:T(8,128)(2,1)} %all-gather.6.cloned.1.call-done), kind=kOutput, calls=%fused_computation.28 | convolution fusion | flops 3221618688 | bytes 11272192 | tf_op jit(solution)/shard_map/dot_general | solution.py:26
  138.9 0.2 reshape.286
  139.1 0.0 copy-done.3
  139.1 0.0 copy-done.4
  139.1 0.5 fusion.43
  139.6 10.5 %bitcast_reduce_fusion = (f32[6,4,128]{2,1,0:T(4,128)S(1)}, f32[2048,6,128,4]{2,0,3,1:T(8,128)}) fusion(pred[2048]{0:T(1024)(128)(4,1)S(1)} %fusion.26, bf16[2048,128,1,1]{1,0,3,2:T(8,128)(2,1)S(1)} %bitcast.148, bf16[6,128,4,128]{3,2,1,0:T(4,128)(2,1)S(1)} %reshape.286), kind=kOutput, calls=%fused_computation.4 | convolution fusion | flops 1629484032 | bytes 26490880 | tf_op jit(solution)/shard_map/stkgd,ukd->skgtu/dot_general | solution.py:62
  150.2 11.4 %fusion.3 = f32[128,6,4,128]{3,0,2,1:T(8,128)S(1)} fusion(bf16[2048,128,1,1]{1,0,3,2:T(8,128)(2,1)S(1)} %bitcast.147, f32[2048,6,128,4]{2,0,3,1:T(8,128)} %get-tuple-element.19, f32[6,4,128]{2,1,0:T(4,128)S(1)} %add.118, pred[2048]{0:T(1024)(128)(4,1)S(1)} %fusion.26), kind=kOutput, calls=%fused_computation.11 | convolution fusion | flops 1635778560 | bytes 27277312 | tf_op jit(solution)/shard_map/skgtu,ukd->stkgd/dot_general | solution.py:76
  161.6 0.0 copy-done.2
  161.6 0.4 fusion.12
  162.0 0.6 copy.85
  162.6 25.1 %all-gather.8.cloned.1.call-done = bf16[512,4096]{1,0:T(8,128)(2,1)} async-done(((bf16[512,128]{1,0:T(8,128)(2,1)}), bf16[512,4096]{1,0:T(8,128)(2,1)}) %all-gather.8.cloned.1.call-update) | async-done | bytes 4194320 | tf_op jit(solution)/shard_map/all_gather | solution.py:81
  187.7 7.4 %convolution_convert_fusion = bf16[768,4096]{1,0:T(8,128)(2,1)} fusion(bf16[512,4096]{1,0:T(8,128)(2,1)} %all-gather.8.cloned.1.call-done, bf16[96,8,4,128]{3,2,1,0:T(4,128)(2,1)S(1)} %bitcast.146), kind=kOutput, calls=%fused_computation.20 | convolution fusion | flops 3224371200 | bytes 11272192 | tf_op jit(solution)/shard_map/dot_general | solution.py:80
  195.2 0.0 all-reduce.3.cloned.1.call-update
  195.2 0.7 copy-done.5
  195.9 0.1 constant_dynamic-slice_fusion
  195.9 0.1 copy.86
  196.0 0.0 copy-done.9
  196.0 0.6 dynamic-slice.1
  197.3 0.0 copy-start.8
  197.3 145.7 %all-reduce.3.cloned.1.call-done = bf16[768,4096]{1,0:T(8,128)(2,1)} async-done(((bf16[768,4096]{1,0:T(8,128)(2,1)}), bf16[768,4096]{1,0:T(8,128)(2,1)}) %all-reduce.3.cloned.1.call-update) | async-done | bytes 6291472 | tf_op jit(solution)/shard_map/psum | solution.py:85
  343.0 9.8 %fusion.2 = (f32[768]{0:T(1024)S(1)}, f32[768]{0:T(1024)S(1)}, bf16[768,4096]{1,0:T(8,128)(2,1)}) fusion(f32[4096]{0:T(1024)S(1)} %copy-done.6, bf16[768,4096]{1,0:T(8,128)(2,1)} %all-reduce.3.cloned.1.call-done, bf16[6,128,4096]{2,1,0:T(8,128)(2,1)} %param.8), kind=kLoop, calls=%fused_computation.10 | loop fusion | flops 28310016 | bytes 18896896 | tf_op jit(solution)/shard_map/reduce_sum | solution.py:88
  352.8 0.2 fusion.33
  353.0 0.1 convert_divide_fusion
  353.1 0.1 select_reduce_fusion
  353.2 62.7 %all-reduce = f32[192]{0:T(256)S(1)} all-reduce(f32[192]{0:T(256)S(1)} %select_reduce_fusion), channel_id=2, replica_groups=mesh['dp'=32,'mp'=8] {'dp'}, use_global_device_ids=true, to_apply=%region_10.11.clone | all-reduce | flops 192 | bytes 1536
  415.9 0.6 dynamic-slice_add_fusion
  416.5 2.1 constant_dynamic-slice_fusion.1
  (24 shorter events, 0.2 us)
Async XLA Ops:
  7.2 57.1 %all-gather.4.cloned.1.call-start = ((), (), s32[]{:S(2)}) async-start(), calls=%async_computation.1 | async-start | bytes 2162688 | tf_op jit(solution)/shard_map/all_gather | solution.py:24
  8.7 122.8 %all-gather.6.cloned.1.call-start = ((), (), s32[]{:S(2)}) async-start(), calls=%async_computation.2 | async-start | bytes 4325376 | tf_op jit(solution)/shard_map/all_gather | solution.py:23
  10.4 5.2 %copy-start.1 = (bf16[6,128,4096]{2,1,0:T(8,128)(2,1)S(1)}, bf16[6,128,4096]{2,1,0:T(8,128)(2,1)}, u32[]{:S(2)}) copy-start(bf16[6,128,4096]{2,1,0:T(8,128)(2,1)} %param.8) | copy-start | bytes 18874372
  69.5 9.1 %copy-start = (s32[192]{0:T(256)S(1)}, s32[192]{0:T(256)}, u32[]{:S(2)}) copy-start(s32[192]{0:T(256)} %param.15) | copy-start | bytes 2308
  72.1 34.8 %all-to-all-start = ((bf16[2,32,128,128]{3,2,0,1:T(8,128)(2,1)}), bf16[2,32,128,128]{3,2,0,1:T(8,128)(2,1)S(1)}, u32[]{:S(2)}, u32[]{:S(2)}) async-start(bf16[2,32,128,128]{3,2,0,1:T(8,128)(2,1)} %multiply_bitcast_fusion), calls=%async_computation | async-start | bytes 4194304 | tf_op jit(solution)/shard_map/all_to_all | solution.py:45
  77.2 110.5 %all-gather.8.cloned.1.call-start = ((), (), s32[]{:S(2)}) async-start(), calls=%async_computation.3 | async-start | bytes 4325376 | tf_op jit(solution)/shard_map/all_gather | solution.py:81
  77.9 265.1 %all-reduce.3.cloned.1.call-start = ((), (), s32[]{:S(2)}) async-start(), calls=%async_computation.4 | async-start | bytes 12582912 | tf_op jit(solution)/shard_map/psum | solution.py:85
  79.4 0.5 copy-start.7
  107.9 31.2 %copy-start.3 = (bf16[1,768,128]{2,1,0:T(8,128)(2,1)S(1)}, bf16[1,768,128]{2,1,0:T(8,128)(2,1)}, u32[]{:S(2)}) copy-start(bf16[1,768,128]{2,1,0:T(8,128)(2,1)} %get-tuple-element.15) | copy-start | bytes 589828
  107.9 31.2 %copy-start.4 = (pred[6,128,128]{1,2,0:T(8,128)(4,1)S(1)}, pred[6,128,128]{1,2,0:T(8,128)(4,1)}, u32[]{:S(2)}) copy-start(pred[6,128,128]{1,2,0:T(8,128)(4,1)} %broadcast_and_fusion) | copy-start | bytes 294916
  150.1 11.4 %copy-start.2 = (bf16[1,768,128]{2,1,0:T(8,128)(2,1)S(1)}, bf16[1,768,128]{2,1,0:T(8,128)(2,1)}, u32[]{:S(2)}) copy-start(bf16[1,768,128]{2,1,0:T(8,128)(2,1)} %get-tuple-element.14) | copy-start | bytes 589828
  195.2 0.7 copy-start.5
  195.2 0.9 copy-start.9
  195.2 147.9 %copy-start.6 = (f32[4096]{0:T(1024)S(1)}, f32[4096]{0:T(1024)}, u32[]{:S(2)}) copy-start(f32[4096]{0:T(1024)} %param.13) | copy-start | bytes 49156
  197.3 155.6 %copy-start.8 = (s32[6]{0:T(128)S(1)}, s32[6]{0:T(128)}, u32[]{:S(2)}) copy-start(s32[6]{0:T(128)} %copy-done.7) | copy-start | bytes 76
Sparse Core Ops, SparseCore 0:
  11.2 53.0 all-gather.3
  66.8 64.6 all-gather.5
  134.0 53.6 all-gather.7
  195.3 147.6 all-reduce.2
where the time goes:
time: 427 us; the launch traced here: 425 us
  waiting for transfers between devices  264 us (62%)
  blocking collectives  62.7 us (15%)
  matrix products  42.9 us (10%)
  other arithmetic  24.5 us (6%)
  between operations  14.7 us (3%)
  local copies, waits for them, and re-layouts  10.4 us (2%)
  starting transfers between devices  5.44 us (1%)
    psum x1, waiting for transfers between devices, on_device(): lax.psum(partial_value.astype(jnp.bfloat16), 'mp').astype(jnp.float32)  146 us
    unnamed x1, blocking collectives  62.7 us
    all_gather x1, waiting for transfers between devices, on_device(): lax.all_gather(w_kv, 'dp', axis=0, tiled=True)  43.3 us
    all_to_all x1, waiting for transfers between devices, on_device(): lax.all_to_all(outgoing, 'dp', split_axis=1, concat_axis=1, tiled=True)  25.3 us
    all_gather x1, waiting for transfers between devices, on_device(): lax.all_gather(w_out, 'dp', axis=1, tiled=True)  25.1 us
    all_gather x1, waiting for transfers between devices, on_device(): lax.all_gather(w_query, 'dp', axis=0, tiled=True)  23.6 us
    dot_general x1, matrix products, on_device(): jnp.einsum('skgtu,ukd->stkgd', far_probs, far_vals, preferred_element_typ...  11.4 us
    dot_general x1, matrix products, on_device(): jnp.einsum('stkgd,ukd->skgtu', query, far_keys, preferred_element_type=jn...  10.5 us
  transfers between devices with their start and end apart: 5, of which 5 were waited for; matrix products, arithmetic and copies ran while one was open for 13% of the time, Pallas kernels for 0%

commit v1 on v0

v1 whole, which is shorter than its diff:
```python
import functools
import math

import jax
import jax.numpy as jnp
from jax import lax
from jax.experimental import pallas as pl
from jax.experimental.pallas import tpu as pltpu
from jax.sharding import PartitionSpec as P

HS = 128
V_SCALE = 2.0**-10
F32 = jnp.float32
BF16 = jnp.bfloat16
MESH = pl.DeviceIdType.MESH


def start_copy(src, dst, send_sem, recv_sem, device):
    pltpu.make_async_remote_copy(
        src_ref=src, dst_ref=dst, send_sem=send_sem, recv_sem=recv_sem,
        device_id=device, device_id_type=MESH,
    ).start()


def await_recv(ref, send_sem, recv_sem, device):
    pltpu.make_async_remote_copy(
        src_ref=ref, dst_ref=ref, send_sem=send_sem, recv_sem=recv_sem,
        device_id=device, device_id_type=MESH,
    ).wait_recv()


def await_send(ref, send_sem, recv_sem, device):
    pltpu.make_async_remote_copy(
        src_ref=ref, dst_ref=ref, send_sem=send_sem, recv_sem=recv_sem,
        device_id=device, device_id_type=MESH,
    ).wait_send()


class Gather:
    def __init__(self, part, whole, send_sem, sems, me, mp):
        self.part, self.whole = part, whole
        self.send_sem, self.sems = send_sem, sems
        self.mp = mp
        core = lax.rem(me, 2)
        x = lax.rem(lax.div(me, 2), 4)
        y = lax.div(me, 8)
        first = core == 0
        self.f0 = jnp.where(first, x, y)
        self.g0 = jnp.where(first, y, x)
        self.core = core
        self.fmul = jnp.where(first, 2, 8)
        self.gmul = jnp.where(first, 8, 2)
        self.me = me
        self.sibling = me + 1 - 2 * core
        self.steps = (0, 3, 1, 2)

    def index(self, f, g):
        f = lax.rem(self.f0 + f, 4)
        g = lax.rem(self.g0 + g, 4)
        return f * self.fmul + g * self.gmul + self.core

    def other_index(self, i, k):
        f = lax.rem(self.g0 + self.steps[i], 4)
        g = lax.rem(self.f0 + self.steps[k], 4)
        return f * self.gmul + g * self.fmul + 1 - self.core

    def send(self, block, half, sem, to):
        ref = self.part(block, half)
        start_copy(ref, ref, self.send_sem, self.sems.at[sem], (to, self.mp))

    def recv(self, block, half, sem):
        ref = self.part(block, half)
        await_recv(ref, self.send_sem, self.sems.at[sem], (self.sibling, self.mp))

    def spread(self, i):
        block = self.index(self.steps[i], 0)
        self.send(block, None, 4 + i, self.index(0, 1))
        self.send(block, None, 8 + i, self.index(0, 3))
        self.send(block, None, 20 + 4 * i, self.sibling)

    def begin(self):
        block = self.index(0, 0)
        self.send(block, None, 0, self.index(1, 0))
        self.send(block, None, 1, self.index(3, 0))
        self.spread(0)

    def first_ring(self):
        block = self.index(3, 0)
        self.recv(block, None, 0)
        self.send(block, 0, 2, self.index(1, 0))
        self.spread(1)
        block = self.index(1, 0)
        self.recv(block, None, 1)
        self.send(block, 1, 3, self.index(3, 0))
        self.spread(2)

    def first_ring_far(self):
        block = self.index(2, 0)
        self.recv(block, 0, 2)
        self.recv(block, 1, 3)
        self.spread(3)

    def second_ring(self, i):
        f = self.steps[i]
        block = self.index(f, 3)
        self.recv(block, None, 4 + i)
        self.send(block, 0, 12 + i, self.index(0, 1))
        self.send(block, None, 20 + 4 * i + 1, self.sibling)
        block = self.index(f, 1)
        self.recv(block, None, 8 + i)
        self.send(block, 1, 16 + i, self.index(0, 3))
        self.send(block, None, 20 + 4 * i + 2, self.sibling)

    def second_ring_far(self, i):
        block = self.index(self.steps[i], 2)
        self.recv(block, 0, 12 + i)
        self.recv(block, 1, 16 + i)
        self.send(block, None, 20 + 4 * i + 3, self.sibling)

    def from_sibling(self):
        for i in range(4):
            for k in range(4):
                self.recv(self.other_index(i, k), None, 20 + 4 * i + k)

    def events(self):
        return [
            self.first_ring,
            lambda: self.second_ring(0),
            self.first_ring_far,
            lambda: self.second_ring(1),
            lambda: (self.second_ring(2), self.second_ring_far(0)),
            lambda: (self.second_ring(3), self.second_ring_far(1)),
            lambda: (self.second_ring_far(2), self.second_ring_far(3)),
            self.from_sibling,
        ]

    def end(self):
        await_send(self.whole, self.send_sem, self.sems.at[0], (self.sibling, self.mp))


def kernel(
    n_dp, n_mp, slots, levels,
    hidden, gain, w_query, w_kv, w_out, w_head, wanted, src, anc_len, own_len, lens, hits,
    out, values,
    x, own_hidden, wq, wkv, wo, q, kv, kv_out, kv_in, keys, vals, near_v, near_w, far_w, attn,
    part, half_in, full_in, stat, stats, scores,
    local_sem, send_sem, kv_sem, q_sem, o_sem, a2a_sem, half_sem, full_sem, stat_sem, score_sem,
):
    me = lax.axis_index("dp")
    mp = lax.axis_index("mp")
    width = x.shape[1]
    blk = x.shape[0] // slots
    depth = w_query.shape[0]
    heads = w_query.shape[1] // HS
    share = out.shape[1]
    far = levels * blk

    def dp_at(step):
        return lax.rem(me + step, n_dp)

    def mp_at(step):
        return lax.rem(mp + step, n_mp)

    def kv_part(block, half):
        if half is None:
            return wkv.at[pl.ds(block * depth, depth), :]
        return wkv.at[pl.ds(block * depth + half * (depth // 2), depth // 2), :]

    def q_part(block, half):
        if half is None:
            return wq.at[pl.ds(block * depth, depth), :]
        return wq.at[pl.ds(block * depth + half * (depth // 2), depth // 2), :]

    rows_out = w_out.shape[0]

    def o_part(block, half):
        if half is None:
            return wo.at[block]
        return wo.at[block, pl.ds(half * (rows_out // 2), rows_out // 2), :]

    own_copies = [
        pltpu.make_async_copy(w_kv, kv_part(me, None), local_sem.at[0]),
        pltpu.make_async_copy(w_query, q_part(me, None), local_sem.at[1]),
        pltpu.make_async_copy(w_out, o_part(me, None), local_sem.at[2]),
    ]
    hidden_copies = [
        pltpu.make_async_copy(hidden.at[s], x.at[pl.ds(s * blk, blk), :], local_sem.at[4 + s])
        for s in range(slots)
    ]
    column = pl.multiple_of(mp * share, share)
    slice_copy = pltpu.make_async_copy(
        hidden.at[:, :, pl.ds(column, share)], own_hidden, local_sem.at[3]
    )
    for copy in own_copies + hidden_copies + [slice_copy]:
        copy.start()

    barrier = pltpu.get_barrier_semaphore()

    def greet_dp(step, carry):
        pl.semaphore_signal(barrier, inc=1, device_id=(dp_at(step), mp), device_id_type=MESH)
        return carry

    def greet_mp(step, carry):
        pl.semaphore_signal(barrier, inc=1, device_id=(me, mp_at(step)), device_id_type=MESH)
        return carry

    lax.fori_loop(1, n_dp, greet_dp, 0)
    lax.fori_loop(1, n_mp, greet_mp, 0)
    pl.semaphore_wait(barrier, n_dp - 1 + n_mp - 1)

    g_kv = Gather(
        kv_part, wkv.at[pl.ds(0, (n_dp - 1) * depth), :], send_sem.at[0], kv_sem, me, mp
    )
    g_q = Gather(q_part, wq.at[pl.ds(0, (n_dp - 1) * depth), :], send_sem.at[1], q_sem, me, mp)
    g_o = Gather(o_part, wo.at[pl.ds(0, n_dp - 1)], send_sem.at[2], o_sem, me, mp)

    own_copies[0].wait()
    g_kv.begin()

    def norm_segment(s):
        def rows_step(r, carry):
            rows = pl.ds(pl.multiple_of(s * blk + r * 16, 16), 16)
            floats = x[rows, :].astype(F32)
            meansq = jnp.mean(floats * floats, axis=-1, keepdims=True)
            scaled = floats * lax.rsqrt(meansq + 1e-05)
            x[rows, :] = (scaled * gain[...].astype(F32)).astype(BF16)
            return carry

        lax.fori_loop(0, blk // 16, rows_step, 0)

    kv_events = g_kv.events()
    for s in range(slots):
        hidden_copies[s].wait()
        norm_segment(s)
        kv_events[s]()
    for event in kv_events[slots:]:
        event()
    own_copies[1].wait()
    g_q.begin()

    group = slots // 2

    def kv_step(i, carry):
        rows = pl.ds(pl.multiple_of(i * group * blk, group * blk), group * blk)
        proj = jnp.dot(x[rows, :], wkv[...], preferred_element_type=F32)
        for r in range(group):
            piece = proj[r * blk : (r + 1) * blk]
            kv[i * group + r, :, :HS] = piece[:, :HS].astype(BF16)
            kv[i * group + r, :, HS:] = (piece[:, HS:] * V_SCALE).astype(BF16)
        return carry

    lax.fori_loop(0, slots // group, kv_step, 0)

    def a2a_send(step, carry):
        to = dp_at(step)
        kv_out[step] = kv[wanted[to]]
        start_copy(kv_out.at[step], kv_in.at[me], send_sem.at[3], a2a_sem.at[me], (to, mp))
        return carry

    lax.fori_loop(1, n_dp, a2a_send, 0)
    kv_in[me] = jnp.zeros(kv_in.shape[1:], BF16)

    q_events = g_q.events()
    for event in q_events:
        event()
    own_copies[2].wait()
    g_o.begin()

    q_scale = math.log2(math.e) / HS**0.5

    def q_step(i, carry):
        rows = pl.ds(pl.multiple_of(i * group * blk, group * blk), group * blk)
        proj = jnp.dot(x[rows, :], wq[...], preferred_element_type=F32) * q_scale
        for r in range(group):
            for h in range(heads):
                piece = proj[r * blk : (r + 1) * blk, h * HS : (h + 1) * HS]
                q[i * group + r, h * blk : (h + 1) * blk, :] = piece.astype(BF16)
        return carry

    o_events = g_o.events()
    for event in o_events[:3]:
        event()
    lax.fori_loop(0, slots // group, q_step, 0)
    for event in o_events[3:5]:
        event()

    token = lax.broadcasted_iota(jnp.int32, (blk, HS), 0)

    def masked(block, count):
        floats = block.astype(F32)
        live = token < count
        return (
            jnp.where(live, floats[:, :HS], 0.0).astype(BF16),
            jnp.where(live, floats[:, HS:], 0.0).astype(BF16),
            jnp.where(live, 1.0, 0.0).astype(BF16),
        )

    def near_step(s, carry):
        key, val, ones = masked(kv[s], own_len[s])
        near_v[s, :, :HS] = val
        near_v[s, :, HS:] = ones
        score = lax.dot_general(
            q[s], key, (((1,), (1,)), ((), ())), preferred_element_type=F32
        )
        row = lax.broadcasted_iota(jnp.int32, score.shape, 0) & (blk - 1)
        col = lax.broadcasted_iota(jnp.int32, score.shape, 1)
        near_w[s] = jnp.where(col <= row, jnp.exp2(score), 0.0).astype(BF16)
        return carry

    lax.fori_loop(0, slots, near_step, 0)
    for event in o_events[5:]:
        event()

    def a2a_wait(step, carry):
        source = dp_at(step)
        await_recv(kv_in.at[source], send_sem.at[3], a2a_sem.at[source], (source, mp))
        return carry

    lax.fori_loop(1, n_dp, a2a_wait, 0)

    def far_step(j, carry):
        key, val, ones = masked(kv_in[src[j]], anc_len[j])
        rows = pl.ds(pl.multiple_of(j * blk, blk), blk)
        keys[rows, :] = key
        vals[rows, :HS] = val
        vals[rows, HS:] = ones
        return carry

    lax.fori_loop(0, levels, far_step, 0)

    stat[...] = jnp.zeros(stat.shape, F32)
    chunk = 512
    plus, minus = (me, mp_at(1)), (me, mp_at(n_mp - 1))
    half = blk // 2

    def compute(s):
        def score_step(j, carry):
            cols = pl.ds(pl.multiple_of(j * chunk, chunk), chunk)
            score = lax.dot_general(
                q[s], keys[cols, :], (((1,), (1,)), ((), ())), preferred_element_type=F32
            )
            far_w[:, cols] = jnp.exp2(score).astype(BF16)
            return carry

        lax.fori_loop(0, far // chunk, score_step, 0)
        both = jnp.dot(far_w[...], vals[...], preferred_element_type=F32)
        both = both + jnp.dot(near_w[s], near_v[s], preferred_element_type=F32)
        mean = both[:, :HS] * (1.0 / both[:, HS:]) * (1.0 / V_SCALE)
        for h in range(heads):
            attn[:, h * HS : (h + 1) * HS] = mean[h * blk : (h + 1) * blk].astype(BF16)

        def out_step(j, carry):
            to = mp_at(n_mp // 2 + j)
            per = share // wo.shape[2]
            weight = jnp.concatenate([wo[to * per + i] for i in range(per)], axis=1)
            result = jnp.dot(attn[...], weight, preferred_element_type=F32)
            part[s, to] = result.astype(BF16)
            return carry

        lax.fori_loop(0, n_mp, out_step, 0)

    def send_half(s):
        to = mp_at(n_mp // 2)
        start_copy(
            part.at[s, to, pl.ds(0, half), :], half_in.at[s, 0], send_sem.at[4],
            half_sem.at[2 * s], plus,
        )
        start_copy(
            part.at[s, to, pl.ds(half, half), :], half_in.at[s, 1], send_sem.at[4],
            half_sem.at[2 * s + 1], minus,
        )

    def pass_on(s, hop):
        for side, device in ((0, plus), (1, minus)):
            steps = n_mp // 2 - 1 - hop
            to = mp_at(steps if side == 0 else n_mp - steps)
            if hop == 0:
                await_recv(half_in.at[s, side], send_sem.at[4], half_sem.at[2 * s + side], device)
                rows = pl.ds(side * half, half)
                mine = part[s, to, rows, :].astype(F32)
                part[s, to, rows, :] = (mine + half_in[s, side].astype(F32)).astype(BF16)
            else:
                sem = full_sem.at[(2 * s + side) * 3 + hop - 1]
                await_recv(full_in.at[s, side, hop - 1], send_sem.at[4], sem, device)
                mine = part[s, to].astype(F32)
                part[s, to] = (mine + full_in[s, side, hop - 1].astype(F32)).astype(BF16)
            sem = full_sem.at[(2 * s + side) * 3 + hop]
            start_copy(part.at[s, to], full_in.at[s, side, hop], send_sem.at[4], sem, device)

    def finish(s):
        for side, device in ((0, plus), (1, minus)):
            sem = full_sem.at[(2 * s + side) * 3 + 2]
            await_recv(full_in.at[s, side, 2], send_sem.at[4], sem, device)
        total = part[s, mp].astype(F32) + full_in[s, 0, 2].astype(F32)
        total = total + full_in[s, 1, 2].astype(F32)
        result = (own_hidden[s].astype(F32) + total).astype(BF16)
        out[pl.ds(pl.multiple_of(s * blk, blk), blk), :] = result
        floats = result.astype(F32)
        weighted = floats * w_head[:, pl.ds(column, share)]
        floats = floats * floats
        for base, terms in ((0, floats), (8, weighted)):
            lanes = terms[:, :128]
            for i in range(1, share // 128):
                lanes = lanes + terms[:, i * 128 : (i + 1) * 128]
            stat[pl.ds(base + s, 1), :] = jnp.sum(lanes.T, axis=0, keepdims=True)

    slice_copy.wait()

    def stage(t, carry):
        for late, act in (
            (4, finish),
            (3, lambda s: pass_on(s, 2)),
            (2, lambda s: pass_on(s, 1)),
            (1, lambda s: pass_on(s, 0)),
        ):
            s = t - late

            @pl.when((s >= 0) & (s < slots))
            def _():
                act(s)

        @pl.when(t < slots)
        def _():
            compute(t)
            send_half(t)

        return carry

    lax.fori_loop(0, slots + 4, stage, 0)

    def stat_send(step, carry):
        start_copy(stat, stats.at[mp], send_sem.at[5], stat_sem.at[mp], (me, mp_at(step)))
        return carry

    def stat_wait(step, carry):
        source = mp_at(step)
        await_recv(stats.at[source], send_sem.at[5], stat_sem.at[source], (me, source))
        return carry

    lax.fori_loop(1, n_mp, stat_send, 0)
    stats[mp] = stat[...]
    lax.fori_loop(1, n_mp, stat_wait, 0)
    sums = jnp.sum(stats[...], axis=0)
    token_score = sums[8:] * lax.rsqrt(sums[:8] / width + 1e-05)
    place = lax.broadcasted_iota(jnp.int32, token_score.shape, 1)
    used = place < lens[...]
    node = jnp.sum(jnp.where(used, token_score, 0.0), axis=1, keepdims=True)
    node = jnp.broadcast_to(node, token_score.shape) / lens[...].astype(F32)
    scores[me] = jnp.broadcast_to(jnp.sum(node, axis=0, keepdims=True), node.shape)

    def score_send(step, carry):
        start_copy(
            scores.at[me], scores.at[me], send_sem.at[6], score_sem.at[me], (dp_at(step), mp)
        )
        return carry

    def score_wait(step, carry):
        source = dp_at(step)
        await_recv(scores.at[source], send_sem.at[6], score_sem.at[source], (source, mp))
        return carry

    lax.fori_loop(1, n_dp, score_send, 0)
    lax.fori_loop(1, n_dp, score_wait, 0)
    values[...] = node + jnp.sum(hits[...] * scores[...], axis=0)

    g_kv.end()
    g_q.end()
    g_o.end()
    await_send(kv_out.at[pl.ds(0, n_dp - 1)], send_sem.at[3], a2a_sem.at[0], plus)
    await_send(part.at[:, pl.ds(0, n_mp - 1)], send_sem.at[4], half_sem.at[0], plus)
    await_send(stats.at[pl.ds(0, n_mp - 1)], send_sem.at[5], stat_sem.at[0], plus)
    await_send(scores.at[pl.ds(0, n_dp - 1)], send_sem.at[6], score_sem.at[0], plus)


def on_device(hidden, norm_gain, w_query, w_kv, w_out, w_head, parents, lengths):
    slots, blk, width = hidden.shape
    n_dp, n_mp = lax.axis_size("dp"), lax.axis_size("mp")
    levels = parents.shape[1]
    depth, q_columns = w_query.shape
    heads = q_columns // HS
    share = width // n_mp
    me = lax.axis_index("dp")
    w_kv = w_kv.reshape(depth, -1)
    kv_columns = w_kv.shape[1]
    firsts = parents.reshape(n_dp, slots, levels)[:, 0, :]
    mine_hit = (firsts >= me * slots) & (firsts < (me + 1) * slots)
    wanted = jnp.sum(jnp.where(mine_hit, firsts - me * slots, 0), axis=1).astype(jnp.int32)
    chain = lax.dynamic_index_in_dim(firsts, me, 0, keepdims=False)
    safe = jnp.maximum(chain, 0)
    anc_len = jnp.where(chain >= 0, jnp.take(lengths, safe), 0)
    src = safe // slots
    own_len = lax.dynamic_slice_in_dim(lengths, me * slots, slots)
    lens = jnp.concatenate([own_len, jnp.ones((8 - slots,), jnp.int32)])
    lens = jnp.broadcast_to(lens[:, None], (8, 128))
    own_nodes = me * slots + jnp.arange(8, dtype=jnp.int32)
    hits = jnp.any(firsts[:, None, :] == own_nodes[None, :, None], axis=2)
    hits = jnp.broadcast_to(hits.astype(F32)[:, :, None], (n_dp, 8, 128))
    any_space = pl.BlockSpec(memory_space=pl.ANY)
    vmem = pl.BlockSpec(memory_space=pltpu.VMEM)
    smem = pl.BlockSpec(memory_space=pltpu.SMEM)
    dma = pltpu.SemaphoreType.DMA
    far = levels * blk
    layer, values = pl.pallas_call(
        functools.partial(kernel, n_dp, n_mp, slots, levels),
        out_shape=(
            jax.ShapeDtypeStruct((slots * blk, share), BF16),
            jax.ShapeDtypeStruct((8, 128), F32),
        ),
        in_specs=[any_space, vmem, any_space, any_space, any_space, vmem]
        + [smem] * 4
        + [vmem] * 2,
        out_specs=(vmem, vmem),
        scratch_shapes=[
            pltpu.VMEM((slots * blk, width), BF16),
            pltpu.VMEM((slots, blk, share), BF16),
            pltpu.VMEM((width, q_columns), BF16),
            pltpu.VMEM((width, kv_columns), BF16),
            pltpu.VMEM((n_dp,) + w_out.shape, BF16),
            pltpu.VMEM((slots, heads * blk, HS), BF16),
            pltpu.VMEM((slots, blk, kv_columns), BF16),
            pltpu.VMEM((n_dp, blk, kv_columns), BF16),
            pltpu.VMEM((n_dp, blk, kv_columns), BF16),
            pltpu.VMEM((far, HS), BF16),
            pltpu.VMEM((far, 2 * HS), BF16),
            pltpu.VMEM((slots, blk, 2 * HS), BF16),
            pltpu.VMEM((slots, heads * blk, blk), BF16),
            pltpu.VMEM((heads * blk, far), BF16),
            pltpu.VMEM((blk, q_columns), BF16),
            pltpu.VMEM((slots, n_mp, blk, share), BF16),
            pltpu.VMEM((slots, 2, blk // 2, share), BF16),
            pltpu.VMEM((slots, 2, 3, blk, share), BF16),
            pltpu.VMEM((16, 128), F32),
            pltpu.VMEM((n_mp, 16, 128), F32),
            pltpu.VMEM((n_dp, 8, 128), F32),
            dma((4 + slots,)),
            dma((7,)),
            dma((36,)),
            dma((36,)),
            dma((36,)),
            dma((n_dp,)),
            dma((2 * slots,)),
            dma((6 * slots,)),
            dma((n_mp,)),
            dma((n_dp,)),
        ],
        compiler_params=pltpu.CompilerParams(
            collective_id=0, has_side_effects=True, vmem_limit_bytes=60 * 1024 * 1024
        ),
    )(
        hidden, norm_gain.reshape(1, width), w_query, w_kv, w_out, w_head.reshape(1, width),
        wanted, src, anc_len, own_len, lens, hits,
    )
    return layer.reshape(slots, blk, share), values[:slots, 0]


def solution(mesh):
    in_specs = (
        P("dp", None, None),
        P(),
        P("dp", "mp"),
        P("dp", None, "mp"),
        P("mp", "dp"),
        P(),
        P(),
        P(),
    )
    out_specs = (P("dp", None, "mp"), P("dp"))
    return jax.shard_map(
        on_device, mesh=mesh, in_specs=in_specs, out_specs=out_specs, check_vma=False
    )
```

time: 427 us -> 189 us (0.44)
  waiting for transfers between devices: 264 us -> 0 us
  Pallas kernels: 0 us -> 176 us
  blocking collectives: 62.7 us -> 0 us
  matrix products: 42.9 us -> 0 us
  other arithmetic: 24.5 us -> 1.34 us
  between operations: 14.7 us -> 0.68 us
  starting transfers between devices: 5.44 us -> 0 us
    pallas_call x0 -> x1, Pallas kernels: none -> 176 us  [on_device(): pl.pallas_call(functools.partial(kernel, n_dp, n_mp, slots, levels), out_...]
    psum x1 -> x0, waiting for transfers between devices: 146 us -> none  [on_device(): lax.psum(partial_value.astype(jnp.bfloat16), 'mp').astype(jnp.float32)]
    all_gather x3 -> x0, waiting for transfers between devices: 92 us -> none  [the longest x1 43.3 us: on_device(): lax.all_gather(w_kv, 'dp', axis=0, tiled=True)]
    unnamed x1 -> x0, blocking collectives: 62.7 us -> none
    dot_general x7 -> x0, matrix products: 42.9 us -> none  [the longest x1 11.4 us: on_device(): jnp.einsum('skgtu,ukd->stkgd', far_probs, far_vals, preferred_element_typ...]
    all_to_all x1 -> x0, waiting for transfers between devices: 25.3 us -> none  [on_device(): lax.all_to_all(outgoing, 'dp', split_axis=1, concat_axis=1, tiled=True)]
    reduce_sum x5 -> x1, other arithmetic: 14.4 us -> 0.63 us  [on_device(): jnp.sum(jnp.where(mine_hit, firsts - me * slots, 0), axis=1)]
    convert_element_type x3 -> x1, other arithmetic: 6.24 us -> 0.01 us  [on_device(): hits = jnp.broadcast_to(hits.astype(F32)[:, :, None], (n_dp, 8, 128))]
  transfers between devices with their start and end apart: 5 -> 0, of which waited for: 5 -> 0; matrix products, arithmetic and copies ran while one was open for 13% -> 0% of each run, Pallas kernels for 0% -> 0%
where the time goes in v1:
time: 189 us; the launch traced here: 188 us
  Pallas kernels  176 us (93%)
  local copies, waits for them, and re-layouts  10.7 us (6%)
    pallas_call x1, Pallas kernels, on_device(): pl.pallas_call(functools.partial(kernel, n_dp, n_mp, slots, levels), out_...  176 us
    unnamed x5, local copies, waits for them, and re-layouts  4.38 us

profile of v1, /device:TPU:1, one launch (start us, length us, event | category | flops | bytes accessed | tf_op | source)
XLA Modules:
  0.0 188.5 jit_solution(6953573526556741594)
XLA Ops:
  0.6 0.8 dynamic_slice.8.own_len
  1.4 0.0 copy-start
  1.4 0.7 broadcast_in_dim.13.lens
  2.1 1.3 reshape.63.gain
  3.4 1.5 copy.17
  4.8 0.8 copy.12
  5.7 0.6 select_reduce_fusion.wanted
  6.3 1.3 gather_fusion
  7.7 0.6 bitcast_select_fusion.1
  8.3 0.1 copy.13
  8.3 0.1 compare_reduce_fusion
  8.5 0.1 copy.14
  8.5 0.8 broadcast_in_dim.14.hits
  9.3 0.0 copy-done
  9.3 175.8 %shard_map.95 = (bf16[768,512]{1,0:T(8,128)(2,1)}, f32[8,128]{1,0:T(8,128)}) custom-call(bf16[6,128,4096]{2,1,0:T(8,128)(2,1)} %hidden.1, bf16[1,4096]{1,0:T(2,128)(2,1)} %reshape.63.gain, bf16[128,512]{1,0:T(8,128)(2,1)} %w_query.1, bf16[128,256]{1,0:T(8,128)(2,1)} %bitcast.20, bf16[512,128]{1,0:T(8,128)(2,1)} %w_out.1, f32[1,4096]{1,0:T(1,128)} %bitcast.24, ...), custom_call_target="tpu_custom_call" | custom-call | tf_op jit(solution)/shard_map/pallas_call | solution.py:503
  185.1 1.3 slice_reduce_fusion
  186.4 2.1 %copy.19 = bf16[6,128,512]{2,1,0:T(8,128)(2,1)} copy(bf16[6,128,512]{2,1,0:T(8,128)(2,1)} %bitcast.19) | data formatting | bytes 1572864
  (7 shorter events, 0.1 us)
Async XLA Ops:
  1.4 7.9 %copy-start = (s32[6]{0:T(128)}, s32[6]{0:T(128)S(1)}, u32[]{:S(2)}) copy-start(s32[6]{0:T(128)S(1)} %dynamic_slice.8.own_len) | copy-start | bytes 76

commit v2 on v1

v2 whole, which is shorter than its diff:
```python
import functools
import math

import jax
import jax.numpy as jnp
from jax import lax
from jax.experimental import pallas as pl
from jax.experimental.pallas import tpu as pltpu
from jax.sharding import PartitionSpec as P

HS = 128
V_SCALE = 2.0**-10
F32 = jnp.float32
BF16 = jnp.bfloat16
MESH = pl.DeviceIdType.MESH


def start_copy(src, dst, send_sem, recv_sem, device):
    pltpu.make_async_remote_copy(
        src_ref=src, dst_ref=dst, send_sem=send_sem, recv_sem=recv_sem,
        device_id=device, device_id_type=MESH,
    ).start()


def await_recv(ref, send_sem, recv_sem, device):
    pltpu.make_async_remote_copy(
        src_ref=ref, dst_ref=ref, send_sem=send_sem, recv_sem=recv_sem,
        device_id=device, device_id_type=MESH,
    ).wait_recv()


def await_send(ref, send_sem, recv_sem, device):
    pltpu.make_async_remote_copy(
        src_ref=ref, dst_ref=ref, send_sem=send_sem, recv_sem=recv_sem,
        device_id=device, device_id_type=MESH,
    ).wait_send()


class Gather:
    def __init__(self, whole, send_sems, sems, me, mp):
        self.whole, self.send_sems, self.sems = whole, send_sems, sems
        self.mp = mp
        self.core = lax.rem(me, 2)
        self.x = lax.rem(lax.div(me, 2), 4)
        self.y = lax.div(me, 8)
        self.sibling = me + 1 - 2 * self.core

    def device(self, first, second):
        on_x = jnp.where(self.core == 0, first, second)
        on_y = jnp.where(self.core == 0, second, first)
        return lax.rem(self.y + on_y, 4) * 8 + lax.rem(self.x + on_x, 4) * 2 + self.core

    def block(self, back):
        on_x = jnp.where(self.core == 0, 4 - back, 0)
        on_y = jnp.where(self.core == 0, 0, 4 - back)
        return self.whole.at[lax.rem(self.y + on_y, 4), lax.rem(self.x + on_x, 4), self.core]

    def line(self, core, back):
        if core == 0:
            return self.whole.at[lax.rem(self.y + 4 - back, 4), :, 0]
        return self.whole.at[:, lax.rem(self.x + 4 - back, 4), 1]

    def per_core(self, act):
        for core in range(2):
            @pl.when(self.core == core)
            def _():
                act(core)

    def copy(self, ref, sem, to):
        return pltpu.make_async_remote_copy(
            src_ref=ref, dst_ref=ref, send_sem=self.send_sems.at[sem],
            recv_sem=self.sems.at[sem], device_id=(to, self.mp), device_id_type=MESH,
        )

    def begin(self):
        for step in (1, 3, 2):
            self.copy(self.block(0), step - 1, self.device(step, 0)).start()

    def first_done(self):
        for step in (1, 3, 2):
            self.copy(self.block(step), step - 1, self.sibling).wait_recv()

        def act(core):
            for step in (1, 3, 2):
                self.copy(self.line(core, 0), 2 + step, self.device(0, step)).start()
            self.copy(self.line(core, 0), 6, self.sibling).start()

        self.per_core(act)

    def second_done(self):
        def act(core):
            for step in (1, 3, 2):
                self.copy(self.line(core, step), 2 + step, self.sibling).wait_recv()
                self.copy(self.line(core, step), 6 + step, self.sibling).start()

        self.per_core(act)

    def all_done(self):
        def act(core):
            for step in (0, 1, 3, 2):
                self.copy(self.line(1 - core, step), 6 + step, self.sibling).wait_recv()

        self.per_core(act)

    def end(self):
        def act(core):
            for step in range(3, 10):
                self.copy(self.line(core, 0), step, self.sibling).wait_send()

        for step in range(3):
            self.copy(self.block(0), step, self.sibling).wait_send()
        self.per_core(act)


def kernel(
    n_dp, n_mp, slots, levels,
    hidden, gain, w_query, w_kv, w_out, w_head, parents, lengths,
    out, values,
    x, own_hidden, wq, wkv, wo, kv_own, gains, q, kv, kv_out, kv_in, keys, vals, near_v, near_w, far_w,
    attn, partial, stat, stats, scores, wanted,
    local_sem, kv_send, q_send, o_send, kv_sem, q_sem, o_sem, sort_sem, send_sem, a2a_sem,
    attn_sem, stat_sem, score_sem,
):
    me = lax.axis_index("dp")
    mp = lax.axis_index("mp")
    width = x.shape[1]
    blk = x.shape[0] // slots
    heads = wq.shape[-1] // HS
    share = out.shape[1]
    far = levels * blk
    core = lax.rem(me, 2)
    chip_x = lax.rem(lax.div(me, 2), 4)
    chip_y = lax.div(me, 8)
    first_node = me * slots

    def dp_at(step):
        return lax.rem(me + step, n_dp)

    def mp_at(step):
        return lax.rem(mp + step, n_mp)

    sort_to = (lax.rem(me, 4) * 8 + mp, lax.div(me, 4))
    sort_from = (mp * 4 + lax.div(me, 8), lax.rem(me, 8))
    stays = (sort_to[0] == me) & (sort_to[1] == mp)

    kv_copy = pltpu.make_async_copy(w_kv, kv_own, local_sem.at[0])
    q_copy = pltpu.make_async_copy(w_query, wq.at[chip_y, chip_x, core], local_sem.at[1])
    hidden_copies = [
        pltpu.make_async_copy(hidden.at[s], x.at[pl.ds(s * blk, blk), :], local_sem.at[4 + s])
        for s in range(slots)
    ]
    column = pl.multiple_of(mp * share, share)
    slice_copy = pltpu.make_async_copy(
        hidden.at[:, :, pl.ds(column, share)], own_hidden, local_sem.at[3]
    )
    kv_copy.start()
    for copy in hidden_copies:
        copy.start()
    q_copy.start()
    slice_copy.start()

    barrier = pltpu.get_barrier_semaphore()

    def greet(device):
        pl.semaphore_signal(barrier, inc=1, device_id=device, device_id_type=MESH)

    def greet_dp(step, carry):
        greet((dp_at(step), mp))
        return carry

    def greet_mp(step, carry):
        greet((me, mp_at(step)))
        return carry

    lax.fori_loop(1, n_dp, greet_dp, 0)
    lax.fori_loop(1, n_mp, greet_mp, 0)

    @pl.when(jnp.logical_not(stays))
    def _():
        greet(sort_to)
        greet(sort_from)

    g_kv = Gather(wkv, kv_send, kv_sem, me, mp)
    g_q = Gather(wq, q_send, q_sem, me, mp)
    g_o = Gather(wo, o_send, o_sem, me, mp)

    for i in range(width // HS):
        gains[:, i * HS : (i + 1) * HS] = gain[i : i + 1, :].astype(F32)

    def norm_segment(s):
        hidden_copies[s].wait()

        def rows_step(r, carry):
            rows = pl.ds(pl.multiple_of(s * blk + r * 16, 16), 16)
            floats = x[rows, :].astype(F32)
            meansq = jnp.mean(floats * floats, axis=-1, keepdims=True)
            scaled = floats * lax.rsqrt(meansq + 1e-05)
            x[rows, :] = (scaled * gains[...]).astype(BF16)
            return carry

        lax.fori_loop(0, blk // 16, rows_step, 0)

    kv_copy.wait()
    wkv[chip_y, chip_x, core, :, :HS] = kv_own[:, 0, :]
    wkv[chip_y, chip_x, core, :, HS:] = kv_own[:, 1, :]
    norm_segment(0)
    norm_segment(1)
    pl.semaphore_wait(barrier, jnp.where(stays, n_dp + n_mp - 2, n_dp + n_mp))

    g_kv.begin()
    norm_segment(2)
    norm_segment(3)
    g_kv.first_done()
    q_copy.wait()
    g_q.begin()
    norm_segment(4)
    norm_segment(5)

    def want_step(d, carry):
        slot = jnp.int32(-1)
        for j in range(levels):
            place = parents[j, d * slots] - first_node
            slot = jnp.where((place >= 0) & (place < slots), place, slot)
        wanted[d] = slot
        return carry

    lax.fori_loop(0, n_dp, want_step, 0)
    g_kv.second_done()
    g_q.first_done()
    g_kv.all_done()

    group = slots // 2

    def kv_step(i, carry):
        rows = pl.ds(pl.multiple_of(i * group * blk, group * blk), group * blk)
        weight = wkv[...].reshape(width, 2 * HS)
        proj = jnp.dot(x[rows, :], weight, preferred_element_type=F32)
        for r in range(group):
            piece = proj[r * blk : (r + 1) * blk]
            kv[i * group + r, :, :HS] = piece[:, :HS].astype(BF16)
            kv[i * group + r, :, HS:] = (piece[:, HS:] * V_SCALE).astype(BF16)
        return carry

    lax.fori_loop(0, slots // group, kv_step, 0)

    order = ((1, 0), (3, 0), (0, 1), (0, 3), (2, 0), (0, 2), (1, 1), (3, 3))
    order += ((1, 3), (3, 1), (2, 1), (1, 2), (2, 3), (3, 2), (2, 2), (0, 0))
    steps = [(dx, dy, 0) for dx, dy in order[:-1]] + [(dx, dy, 1) for dx, dy in order]
    for i, (dx, dy, flip) in enumerate(steps):
        to = lax.rem(chip_y + dy, 4) * 8 + lax.rem(chip_x + dx, 4) * 2 + lax.rem(core + flip, 2)
        kv_out[i] = kv[jnp.maximum(wanted[to], 0)]
        start_copy(kv_out.at[i], kv_in.at[me], send_sem.at[0], a2a_sem.at[me], (to, mp))
    kv_in[me] = jnp.zeros(kv_in.shape[1:], BF16)

    sort_slot = wo.at[lax.rem(me, 4), lax.div(mp, 2), lax.rem(mp, 2)]
    local_sort = pltpu.make_async_copy(w_out, sort_slot, local_sem.at[2])

    @pl.when(stays)
    def _():
        local_sort.start()

    @pl.when(jnp.logical_not(stays))
    def _():
        start_copy(w_out, sort_slot, sort_sem.at[0], sort_sem.at[1], sort_to)

    g_q.second_done()
    g_q.all_done()

    q_scale = math.log2(math.e) / HS**0.5

    def q_step(i, carry):
        rows = pl.ds(pl.multiple_of(i * group * blk, group * blk), group * blk)
        weight = wq[...].reshape(width, heads * HS)
        proj = jnp.dot(x[rows, :], weight, preferred_element_type=F32) * q_scale
        for r in range(group):
            for h in range(heads):
                piece = proj[r * blk : (r + 1) * blk, h * HS : (h + 1) * HS]
                q[i * group + r, h * blk : (h + 1) * blk, :] = piece.astype(BF16)
        return carry

    lax.fori_loop(0, slots // group, q_step, 0)

    token = lax.broadcasted_iota(jnp.int32, (blk, HS), 0)

    def masked(block, count):
        floats = block.astype(F32)
        live = token < count
        return (
            jnp.where(live, floats[:, :HS], 0.0).astype(BF16),
            jnp.where(live, floats[:, HS:], 0.0).astype(BF16),
            jnp.where(live, 1.0, 0.0).astype(BF16),
        )

    def near_step(s, carry):
        key, val, ones = masked(kv[s], lengths[first_node + s])
        near_v[s, :, :HS] = val
        near_v[s, :, HS:] = ones
        score = lax.dot_general(
            q[s], key, (((1,), (1,)), ((), ())), preferred_element_type=F32
        )
        row = lax.broadcasted_iota(jnp.int32, score.shape, 0) & (blk - 1)
        col = lax.broadcasted_iota(jnp.int32, score.shape, 1)
        near_w[s] = jnp.where(col <= row, jnp.exp2(score), 0.0).astype(BF16)
        return carry

    lax.fori_loop(0, slots, near_step, 0)
    stat[...] = jnp.zeros(stat.shape, F32)
    slice_copy.wait()
    g_kv.end()

    def a2a_wait(step, carry):
        source = dp_at(step)
        await_recv(kv_in.at[source], send_sem.at[0], a2a_sem.at[source], (source, mp))
        return carry

    lax.fori_loop(1, n_dp, a2a_wait, 0)

    @pl.when(stays)
    def _():
        local_sort.wait()

    @pl.when(jnp.logical_not(stays))
    def _():
        own_slot = wo.at[chip_y, chip_x, core]
        await_recv(own_slot, sort_sem.at[0], sort_sem.at[1], sort_from)

    g_o.begin()

    def far_step(j, carry):
        node = parents[j, first_node]
        safe = jnp.maximum(node, 0)
        count = jnp.where(node >= 0, lengths[safe], 0)
        key, val, ones = masked(kv_in[lax.div(safe, slots)], count)
        rows = pl.ds(pl.multiple_of(j * blk, blk), blk)
        keys[rows, :] = key
        vals[rows, :HS] = val
        vals[rows, HS:] = ones
        return carry

    lax.fori_loop(0, levels, far_step, 0)

    chunk = 512
    plus, minus = (me, mp_at(1)), (me, mp_at(n_mp - 1))
    sides = ((0, plus, n_mp - 1), (1, minus, 1))
    half = blk // 2

    def attend(s):
        def score_step(j, carry):
            cols = pl.ds(pl.multiple_of(j * chunk, chunk), chunk)
            score = lax.dot_general(
                q[s], keys[cols, :], (((1,), (1,)), ((), ())), preferred_element_type=F32
            )
            far_w[:, cols] = jnp.exp2(score).astype(BF16)
            return carry

        lax.fori_loop(0, far // chunk, score_step, 0)
        both = jnp.dot(far_w[...], vals[...], preferred_element_type=F32)
        both = both + jnp.dot(near_w[s], near_v[s], preferred_element_type=F32)
        mean = both[:, :HS] * (1.0 / both[:, HS:]) * (1.0 / V_SCALE)
        for h in range(heads):
            attn[s, mp, :, h * HS : (h + 1) * HS] = mean[h * blk : (h + 1) * blk].astype(BF16)

    def attn_part(s, side, hop):
        source = mp_at((n_mp - hop) if side == 0 else hop)
        if hop == n_mp // 2:
            return attn.at[s, source, pl.ds(side * half, half), :]
        return attn.at[s, source]

    def attn_sem_at(s, side, hop):
        return attn_sem.at[(s * 2 + side) * (n_mp // 2) + hop - 1]

    def send_on(s, hop):
        for side, device, _ in sides:
            if hop > 0:
                ref = attn_part(s, side, hop)
                await_recv(ref, send_sem.at[1], attn_sem_at(s, side, hop), device)
            source = mp_at((n_mp - hop) if side == 0 else hop)
            ref = attn.at[s, source]
            if hop + 1 == n_mp // 2:
                ref = attn.at[s, source, pl.ds(side * half, half), :]
            start_copy(ref, ref, send_sem.at[1], attn_sem_at(s, side, hop + 1), device)

    def attend_step(s, carry):
        attend(s)
        send_on(s, 0)

        @pl.when(s == 1)
        def _():
            g_o.first_done()

        return carry

    lax.fori_loop(0, slots, attend_step, 0)
    for s in range(slots):
        send_on(s, 1)
    g_o.second_done()
    for s in range(slots):
        send_on(s, 2)
    g_o.all_done()

    def weight_at(sources, pair):
        cols = []
        for j in (2 * pair, 2 * pair + 1):
            rows = [wo[j, lax.div(m, 2), lax.rem(m, 2)] for m in sources]
            cols.append(jnp.concatenate(rows, axis=0) if len(rows) > 1 else rows[0])
        return jnp.concatenate(cols, axis=1)

    opposite = mp_at(n_mp // 2)
    others = [mp_at(i) for i in range(n_mp) if i != n_mp // 2]

    def most(s, carry):
        send_on(s, 3)
        rows = jnp.concatenate([attn[s, m] for m in others], axis=1)
        for pair in range(2):
            cols = slice(pair * 2 * HS, (pair + 1) * 2 * HS)
            partial[s, :, cols] = jnp.dot(
                rows, weight_at(others, pair), preferred_element_type=F32
            )
        return carry

    lax.fori_loop(0, slots, most, 0)

    def finish(s, carry):
        for side, device, _ in sides:
            ref = attn_part(s, side, n_mp // 2)
            await_recv(ref, send_sem.at[1], attn_sem_at(s, side, n_mp // 2), device)
        weight = jnp.concatenate([weight_at([opposite], pair) for pair in range(2)], axis=1)
        total = partial[s] + jnp.dot(attn[s, opposite], weight, preferred_element_type=F32)
        result = (own_hidden[s].astype(F32) + total).astype(BF16)
        out[pl.ds(pl.multiple_of(s * blk, blk), blk), :] = result
        floats = result.astype(F32)
        heads_at = mp * (share // HS)
        head = jnp.concatenate(
            [w_head[pl.ds(heads_at + i, 1), :] for i in range(share // HS)], axis=1
        )
        weighted = floats * head
        floats = floats * floats
        for base, terms in ((0, floats), (8, weighted)):
            lanes = terms[:, :HS]
            for i in range(1, share // HS):
                lanes = lanes + terms[:, i * HS : (i + 1) * HS]
            stat[pl.ds(base + s, 1), :] = jnp.sum(lanes.T, axis=0, keepdims=True)
        return carry

    lax.fori_loop(0, slots, finish, 0)

    def stat_send(step, carry):
        start_copy(stat, stats.at[mp], send_sem.at[2], stat_sem.at[mp], (me, mp_at(step)))
        return carry

    def stat_wait(step, carry):
        source = mp_at(step)
        await_recv(stats.at[source], send_sem.at[2], stat_sem.at[source], (me, source))
        return carry

    lax.fori_loop(1, n_mp, stat_send, 0)
    stats[mp] = stat[...]
    place = lax.broadcasted_iota(jnp.int32, (8, 128), 1)
    row = lax.broadcasted_iota(jnp.int32, (8, 128), 0)
    lens = jnp.ones((8, 128), jnp.int32)
    for s in range(slots):
        lens = jnp.where(row == s, lengths[first_node + s], lens)
    lax.fori_loop(1, n_mp, stat_wait, 0)
    sums = jnp.sum(stats[...], axis=0)
    token_score = sums[8:] * lax.rsqrt(sums[:8] / width + 1e-05)
    node = jnp.sum(jnp.where(place < lens, token_score, 0.0), axis=1, keepdims=True)
    node = jnp.broadcast_to(node, token_score.shape) / lens.astype(F32)
    scores[me] = jnp.broadcast_to(jnp.sum(node, axis=0, keepdims=True), node.shape)

    def score_send(step, carry):
        start_copy(
            scores.at[me], scores.at[me], send_sem.at[3], score_sem.at[me], (dp_at(step), mp)
        )
        return carry

    def score_wait(step, carry):
        source = dp_at(step)
        await_recv(scores.at[source], send_sem.at[3], score_sem.at[source], (source, mp))
        return carry

    lax.fori_loop(1, n_dp, score_send, 0)

    g_q.end()
    g_o.end()

    @pl.when(jnp.logical_not(stays))
    def _():
        await_send(wo.at[chip_y, chip_x, core], sort_sem.at[0], sort_sem.at[1], sort_to)

    await_send(kv_out.at[pl.ds(0, n_dp - 1)], send_sem.at[0], a2a_sem.at[0], plus)
    await_send(attn.at[:, pl.ds(0, n_mp - 1)], send_sem.at[1], attn_sem.at[0], plus)
    await_send(stats.at[pl.ds(0, n_mp - 1)], send_sem.at[2], stat_sem.at[0], plus)
    lax.fori_loop(1, n_dp, score_wait, 0)

    def add_step(d, total):
        return total + jnp.where(row == wanted[d], scores[d], 0.0)

    values[...] = lax.fori_loop(0, n_dp, add_step, node)
    await_send(scores.at[pl.ds(0, n_dp - 1)], send_sem.at[3], score_sem.at[0], plus)


def on_device(hidden, norm_gain, w_query, w_kv, w_out, w_head, parents, lengths):
    slots, blk, width = hidden.shape
    n_dp, n_mp = lax.axis_size("dp"), lax.axis_size("mp")
    levels = parents.shape[1]
    depth, q_columns = w_query.shape
    heads = q_columns // HS
    share = width // n_mp
    any_space = pl.BlockSpec(memory_space=pl.ANY)
    vmem = pl.BlockSpec(memory_space=pltpu.VMEM)
    smem = pl.BlockSpec(memory_space=pltpu.SMEM)
    dma = pltpu.SemaphoreType.DMA
    far = levels * blk
    layer, values = pl.pallas_call(
        functools.partial(kernel, n_dp, n_mp, slots, levels),
        out_shape=(
            jax.ShapeDtypeStruct((slots * blk, share), BF16),
            jax.ShapeDtypeStruct((8, 128), F32),
        ),
        in_specs=[any_space, vmem, any_space, any_space, any_space, vmem, smem, smem],
        out_specs=(vmem, vmem),
        scratch_shapes=[
            pltpu.VMEM((slots * blk, width), BF16),
            pltpu.VMEM((slots, blk, share), BF16),
            pltpu.VMEM((4, 4, 2, depth, q_columns), BF16),
            pltpu.VMEM((4, 4, 2, depth, 2 * HS), BF16),
            pltpu.VMEM((4, 4, 2) + w_out.shape, BF16),
            pltpu.VMEM(w_kv.shape, BF16),
            pltpu.VMEM((1, width), F32),
            pltpu.VMEM((slots, heads * blk, HS), BF16),
            pltpu.VMEM((slots, blk, 2 * HS), BF16),
            pltpu.VMEM((n_dp, blk, 2 * HS), BF16),
            pltpu.VMEM((n_dp, blk, 2 * HS), BF16),
            pltpu.VMEM((far, HS), BF16),
            pltpu.VMEM((far, 2 * HS), BF16),
            pltpu.VMEM((slots, blk, 2 * HS), BF16),
            pltpu.VMEM((slots, heads * blk, blk), BF16),
            pltpu.VMEM((heads * blk, far), BF16),
            pltpu.VMEM((slots, n_mp, blk, q_columns), BF16),
            pltpu.VMEM((slots, blk, share), F32),
            pltpu.VMEM((16, 128), F32),
            pltpu.VMEM((n_mp, 16, 128), F32),
            pltpu.VMEM((n_dp, 8, 128), F32),
            pltpu.SMEM((n_dp,), jnp.int32),
            dma((4 + slots,)),
            dma((10,)),
            dma((10,)),
            dma((10,)),
            dma((10,)),
            dma((10,)),
            dma((10,)),
            dma((2,)),
            dma((4,)),
            dma((n_dp,)),
            dma((slots * n_mp,)),
            dma((n_mp,)),
            dma((n_dp,)),
        ],
        compiler_params=pltpu.CompilerParams(
            collective_id=0, has_side_effects=True, vmem_limit_bytes=60 * 1024 * 1024
        ),
    )(
        hidden, norm_gain.reshape(width // HS, HS), w_query, w_kv, w_out,
        w_head.reshape(width // HS, HS), parents.T, lengths,
    )
    return layer.reshape(slots, blk, share), values[:slots, 0]


def solution(mesh):
    in_specs = (
        P("dp", None, None),
        P(),
        P("dp", "mp"),
        P("dp", None, "mp"),
        P("mp", "dp"),
        P(),
        P(),
        P(),
    )
    out_specs = (P("dp", None, "mp"), P("dp"))
    return jax.shard_map(
        on_device, mesh=mesh, in_specs=in_specs, out_specs=out_specs, check_vma=False
    )
```

time: 189 us -> 159 us (0.84)
  Pallas kernels: 176 us -> 155 us
  local copies, waits for them, and re-layouts: 10.7 us -> 3.4 us
    pallas_call x1, Pallas kernels: 176 us -> 155 us  [on_device(): pl.pallas_call(functools.partial(kernel, n_dp, n_mp, slots, levels), out_...]
    unnamed x5 -> x1, local copies, waits for them, and re-layouts: 4.38 us -> 2.1 us
where the time goes in v2:
time: 159 us
  Pallas kernels  155 us (97%)
  local copies, waits for them, and re-layouts  3.4 us (2%)
    pallas_call x1, Pallas kernels, on_device(): pl.pallas_call(functools.partial(kernel, n_dp, n_mp, slots, levels), out_...  155 us

profile of v2, /device:TPU:1, one launch (start us, length us, event | category | flops | bytes accessed | tf_op | source)
XLA Modules:
  0.0 158.7 jit_solution(17800993218272285474)
XLA Ops:
  0.6 154.6 %shard_map.95 = (bf16[768,512]{1,0:T(8,128)(2,1)}, f32[8,128]{1,0:T(8,128)}) custom-call(bf16[6,128,4096]{2,1,0:T(8,128)(2,1)} %hidden.1, bf16[32,128]{1,0:T(8,128)(2,1)} %bitcast.7, bf16[128,512]{1,0:T(8,128)(2,1)} %w_query.1, bf16[128,2,128]{2,1,0:T(2,128)(2,1)} %w_kv.1, bf16[512,128]{1,0:T(8,128)(2,1)} %w_out.1, f32[32,128]{1,0:T(8,128)} %bitcast.5, ...), custom_call_target="tpu_custom_call" | custom-call | tf_op jit(solution)/shard_map/pallas_call | solution.py:514
  155.3 1.3 slice_reduce_fusion
  156.6 2.1 %copy.11 = bf16[6,128,512]{2,1,0:T(8,128)(2,1)} copy(bf16[6,128,512]{2,1,0:T(8,128)(2,1)} %bitcast.4) | data formatting | bytes 1572864

commit v3 on v2

--- a/solution.py
+++ b/solution.py
@@ -116,10 +116,11 @@
     n_dp, n_mp, slots, levels,
     hidden, gain, w_query, w_kv, w_out, w_head, parents, lengths,
     out, values,
-    x, own_hidden, wq, wkv, wo, kv_own, gains, q, kv, kv_out, kv_in, keys, vals, near_v, near_w, far_w,
-    attn, partial, stat, stats, scores, wanted,
-    local_sem, kv_send, q_send, o_send, kv_sem, q_sem, o_sem, sort_sem, send_sem, a2a_sem,
-    attn_sem, stat_sem, score_sem,
+    x, own_hidden, wq, wkv, wo, kv_own, gains, q, kv, pair_out, pair_in, ring_out, ring_in, column_own,
+    col_out, col_in, table, keys, vals, near_v, near_w, far_w,
+    attn, partial, stat, stats, tallies, tally_in, hits,
+    local_sem, kv_send, q_send, o_send, t_send, kv_sem, q_sem, o_sem, t_sem, sort_sem,
+    route_send, route_sem, send_sem, attn_sem, stat_sem, tally_send, tally_sem,
 ):
     me = lax.axis_index("dp")
     mp = lax.axis_index("mp")
@@ -132,9 +133,6 @@
     chip_x = lax.rem(lax.div(me, 2), 4)
     chip_y = lax.div(me, 8)
     first_node = me * slots
-
-    def dp_at(step):
-        return lax.rem(me + step, n_dp)
 
     def mp_at(step):
         return lax.rem(mp + step, n_mp)
@@ -164,25 +162,24 @@
     def greet(device):
         pl.semaphore_signal(barrier, inc=1, device_id=device, device_id_type=MESH)
 
-    def greet_dp(step, carry):
-        greet((dp_at(step), mp))
-        return carry
-
     def greet_mp(step, carry):
         greet((me, mp_at(step)))
         return carry
 
-    lax.fori_loop(1, n_dp, greet_dp, 0)
+    g_kv = Gather(wkv, kv_send, kv_sem, me, mp)
+    g_q = Gather(wq, q_send, q_sem, me, mp)
+    g_o = Gather(wo, o_send, o_sem, me, mp)
+    g_t = Gather(table, t_send, t_sem, me, mp)
+    for step in (1, 3, 2):
+        greet((g_kv.device(step, 0), mp))
+        greet((g_kv.device(0, step), mp))
+    greet((g_kv.sibling, mp))
     lax.fori_loop(1, n_mp, greet_mp, 0)
 
     @pl.when(jnp.logical_not(stays))
     def _():
         greet(sort_to)
         greet(sort_from)
-
-    g_kv = Gather(wkv, kv_send, kv_sem, me, mp)
-    g_q = Gather(wq, q_send, q_sem, me, mp)
-    g_o = Gather(wo, o_send, o_sem, me, mp)
 
     for i in range(width // HS):
         gains[:, i * HS : (i + 1) * HS] = gain[i : i + 1, :].astype(F32)
@@ -205,7 +202,8 @@
     wkv[chip_y, chip_x, core, :, HS:] = kv_own[:, 1, :]
     norm_segment(0)
     norm_segment(1)
-    pl.semaphore_wait(barrier, jnp.where(stays, n_dp + n_mp - 2, n_dp + n_mp))
+    peers = 7 + n_mp - 1
+    pl.semaphore_wait(barrier, jnp.where(stays, peers, peers + 2))
 
     g_kv.begin()
     norm_segment(2)
@@ -216,15 +214,6 @@
     norm_segment(4)
     norm_segment(5)
 
-    def want_step(d, carry):
-        slot = jnp.int32(-1)
-        for j in range(levels):
-            place = parents[j, d * slots] - first_node
-            slot = jnp.where((place >= 0) & (place < slots), place, slot)
-        wanted[d] = slot
-        return carry
-
-    lax.fori_loop(0, n_dp, want_step, 0)
     g_kv.second_done()
     g_q.first_done()
     g_kv.all_done()
@@ -243,14 +232,76 @@
 
     lax.fori_loop(0, slots // group, kv_step, 0)
 
-    order = ((1, 0), (3, 0), (0, 1), (0, 3), (2, 0), (0, 2), (1, 1), (3, 3))
-    order += ((1, 3), (3, 1), (2, 1), (1, 2), (2, 3), (3, 2), (2, 2), (0, 0))
-    steps = [(dx, dy, 0) for dx, dy in order[:-1]] + [(dx, dy, 1) for dx, dy in order]
-    for i, (dx, dy, flip) in enumerate(steps):
-        to = lax.rem(chip_y + dy, 4) * 8 + lax.rem(chip_x + dx, 4) * 2 + lax.rem(core + flip, 2)
-        kv_out[i] = kv[jnp.maximum(wanted[to], 0)]
-        start_copy(kv_out.at[i], kv_in.at[me], send_sem.at[0], a2a_sem.at[me], (to, mp))
-    kv_in[me] = jnp.zeros(kv_in.shape[1:], BF16)
+    f0 = jnp.where(core == 0, chip_x, chip_y)
+    g0 = jnp.where(core == 0, chip_y, chip_x)
+    f_mul = jnp.where(core == 0, 2, 8)
+    g_mul = jnp.where(core == 0, 8, 2)
+
+    def wanted(device):
+        place = parents[0, device * slots] - first_node
+        found = (place >= 0) & (place < slots)
+        block = kv[jnp.clip(place, 0, slots - 1)]
+        return jnp.where(found, block, jnp.zeros_like(block))
+
+    def at4(value):
+        return lax.rem(value, 4)
+
+    for step in (2, 1, 3, 0):
+        line = at4(g0 + step)
+        for k in range(4):
+            pair_out[step, k] = wanted(line * g_mul + k * f_mul + 1 - core)
+        start_copy(
+            pair_out.at[step], pair_in.at[step], route_send.at[step], route_sem.at[step],
+            (g_kv.sibling, mp),
+        )
+    for step in (2, 1, 3, 0):
+        await_recv(pair_in.at[step], route_send.at[step], route_sem.at[step], (g_kv.sibling, mp))
+        line = at4(f0 + step)
+        target = column_own if step == 0 else ring_out.at[step - 1]
+        for k in range(4):
+            target[k] = wanted(line * f_mul + k * g_mul + core) + pair_in[step, k]
+        if step > 0:
+            start_copy(
+                ring_out.at[step - 1], ring_in.at[step - 1], route_send.at[3 + step],
+                route_sem.at[3 + step], (g_kv.device(step, 0), mp),
+            )
+
+    def route_ring():
+        for step in (1, 3, 2):
+            await_recv(
+                ring_in.at[step - 1], route_send.at[3 + step], route_sem.at[3 + step],
+                (g_kv.sibling, mp),
+            )
+
+        def total(k):
+            return column_own[k] + ring_in[0, k] + ring_in[1, k] + ring_in[2, k]
+
+        for step in (2, 1, 3):
+            col_out[step - 1] = total(at4(g0 + step))
+            start_copy(
+                col_out.at[step - 1], col_in.at[step - 1], route_send.at[6 + step],
+                route_sem.at[6 + step], (g_kv.device(0, step), mp),
+            )
+        table[chip_y, chip_x, core] = total(g0)
+
+    def route_column():
+        for step in (1, 3, 2):
+            await_recv(
+                col_in.at[step - 1], route_send.at[6 + step], route_sem.at[6 + step],
+                (g_kv.sibling, mp),
+            )
+        mine = table[chip_y, chip_x, core] + col_in[0] + col_in[1] + col_in[2]
+        table[chip_y, chip_x, core] = mine
+        g_t.begin()
+
+    def route_end():
+        for step in range(4):
+            await_send(pair_out.at[step], route_send.at[step], route_sem.at[step], plus)
+        for step in range(3):
+            await_send(ring_out.at[step], route_send.at[4 + step], route_sem.at[4 + step], plus)
+            await_send(col_out.at[step], route_send.at[7 + step], route_sem.at[7 + step], plus)
+
+    plus, minus = (me, mp_at(1)), (me, mp_at(n_mp - 1))
 
     sort_slot = wo.at[lax.rem(me, 4), lax.div(mp, 2), lax.rem(mp, 2)]
     local_sort = pltpu.make_async_copy(w_out, sort_slot, local_sem.at[2])
@@ -263,7 +314,9 @@
     def _():
         start_copy(w_out, sort_slot, sort_sem.at[0], sort_sem.at[1], sort_to)
 
+    route_ring()
     g_q.second_done()
+    route_column()
     g_q.all_done()
 
     q_scale = math.log2(math.e) / HS**0.5
@@ -278,7 +331,9 @@
                 q[i * group + r, h * blk : (h + 1) * blk, :] = piece.astype(BF16)
         return carry
 
-    lax.fori_loop(0, slots // group, q_step, 0)
+    lax.fori_loop(0, 1, q_step, 0)
+    g_t.first_done()
+    lax.fori_loop(1, slots // group, q_step, 0)
 
     token = lax.broadcasted_iota(jnp.int32, (blk, HS), 0)
 
@@ -308,12 +363,8 @@
     slice_copy.wait()
     g_kv.end()
 
-    def a2a_wait(step, carry):
-        source = dp_at(step)
-        await_recv(kv_in.at[source], send_sem.at[0], a2a_sem.at[source], (source, mp))
-        return carry
-
-    lax.fori_loop(1, n_dp, a2a_wait, 0)
+    g_t.second_done()
+    g_t.all_done()
 
     @pl.when(stays)
     def _():
@@ -330,7 +381,10 @@
         node = parents[j, first_node]
         safe = jnp.maximum(node, 0)
         count = jnp.where(node >= 0, lengths[safe], 0)
-        key, val, ones = masked(kv_in[lax.div(safe, slots)], count)
+        above = jnp.maximum(parents[jnp.maximum(j - 1, 0), first_node], 0)
+        holder = jnp.where(j == 0, me, lax.div(above, slots))
+        spot = table[lax.div(holder, 8), lax.div(lax.rem(holder, 8), 2), lax.rem(holder, 2)]
+        key, val, ones = masked(spot, count)
         rows = pl.ds(pl.multiple_of(j * blk, blk), blk)
         keys[rows, :] = key
         vals[rows, :HS] = val
@@ -340,7 +394,6 @@
     lax.fori_loop(0, levels, far_step, 0)
 
     chunk = 512
-    plus, minus = (me, mp_at(1)), (me, mp_at(n_mp - 1))
     sides = ((0, plus, n_mp - 1), (1, minus, 1))
     half = blk // 2
 
@@ -373,12 +426,12 @@
         for side, device, _ in sides:
             if hop > 0:
                 ref = attn_part(s, side, hop)
-                await_recv(ref, send_sem.at[1], attn_sem_at(s, side, hop), device)
+                await_recv(ref, send_sem.at[0], attn_sem_at(s, side, hop), device)
             source = mp_at((n_mp - hop) if side == 0 else hop)
             ref = attn.at[s, source]
             if hop + 1 == n_mp // 2:
                 ref = attn.at[s, source, pl.ds(side * half, half), :]
-            start_copy(ref, ref, send_sem.at[1], attn_sem_at(s, side, hop + 1), device)
+            start_copy(ref, ref, send_sem.at[0], attn_sem_at(s, side, hop + 1), device)
 
     def attend_step(s, carry):
         attend(s)
@@ -397,6 +450,27 @@
     for s in range(slots):
         send_on(s, 2)
     g_o.all_done()
+
+    row = lax.broadcasted_iota(jnp.int32, (8, 128), 0)
+    place = lax.broadcasted_iota(jnp.int32, (8, 128), 1)
+
+    def hit_step(d, total):
+        slot = jnp.int32(-1)
+        for j in range(levels):
+            spot = parents[j, d * slots] - first_node
+            slot = jnp.where((spot >= 0) & (spot < slots), spot, slot)
+        return total + jnp.where((row == slot) & (place == d), 1.0, 0.0)
+
+    hits[...] = lax.fori_loop(0, n_dp, hit_step, jnp.zeros((8, 128), F32))
+
+    g_q.end()
+    g_o.end()
+    g_t.end()
+    route_end()
+
+    @pl.when(jnp.logical_not(stays))
+    def _():
+        await_send(wo.at[chip_y, chip_x, core], sort_sem.at[0], sort_sem.at[1], sort_to)
 
     def weight_at(sources, pair):
         cols = []
@@ -423,7 +497,7 @@
     def finish(s, carry):
         for side, device, _ in sides:
             ref = attn_part(s, side, n_mp // 2)
-            await_recv(ref, send_sem.at[1], attn_sem_at(s, side, n_mp // 2), device)
+            await_recv(ref, send_sem.at[0], attn_sem_at(s, side, n_mp // 2), device)
         weight = jnp.concatenate([weight_at([opposite], pair) for pair in range(2)], axis=1)
         total = partial[s] + jnp.dot(attn[s, opposite], weight, preferred_element_type=F32)
         result = (own_hidden[s].astype(F32) + total).astype(BF16)
@@ -445,18 +519,16 @@
     lax.fori_loop(0, slots, finish, 0)
 
     def stat_send(step, carry):
-        start_copy(stat, stats.at[mp], send_sem.at[2], stat_sem.at[mp], (me, mp_at(step)))
+        start_copy(stat, stats.at[mp], send_sem.at[1], stat_sem.at[mp], (me, mp_at(step)))
         return carry
 
     def stat_wait(step, carry):
         source = mp_at(step)
-        await_recv(stats.at[source], send_sem.at[2], stat_sem.at[source], (me, source))
+        await_recv(stats.at[source], send_sem.at[1], stat_sem.at[source], (me, source))
         return carry
 
     lax.fori_loop(1, n_mp, stat_send, 0)
     stats[mp] = stat[...]
-    place = lax.broadcasted_iota(jnp.int32, (8, 128), 1)
-    row = lax.broadcasted_iota(jnp.int32, (8, 128), 0)
     lens = jnp.ones((8, 128), jnp.int32)
     for s in range(slots):
         lens = jnp.where(row == s, lengths[first_node + s], lens)
@@ -465,38 +537,30 @@
     token_score = sums[8:] * lax.rsqrt(sums[:8] / width + 1e-05)
     node = jnp.sum(jnp.where(place < lens, token_score, 0.0), axis=1, keepdims=True)
     node = jnp.broadcast_to(node, token_score.shape) / lens.astype(F32)
-    scores[me] = jnp.broadcast_to(jnp.sum(node, axis=0, keepdims=True), node.shape)
-
-    def score_send(step, carry):
-        start_copy(
-            scores.at[me], scores.at[me], send_sem.at[3], score_sem.at[me], (dp_at(step), mp)
-        )
-        return carry
-
-    def score_wait(step, carry):
-        source = dp_at(step)
-        await_recv(scores.at[source], send_sem.at[3], score_sem.at[source], (source, mp))
-        return carry
-
-    lax.fori_loop(1, n_dp, score_send, 0)
-
-    g_q.end()
-    g_o.end()
-
-    @pl.when(jnp.logical_not(stays))
-    def _():
-        await_send(wo.at[chip_y, chip_x, core], sort_sem.at[0], sort_sem.at[1], sort_to)
-
-    await_send(kv_out.at[pl.ds(0, n_dp - 1)], send_sem.at[0], a2a_sem.at[0], plus)
-    await_send(attn.at[:, pl.ds(0, n_mp - 1)], send_sem.at[1], attn_sem.at[0], plus)
-    await_send(stats.at[pl.ds(0, n_mp - 1)], send_sem.at[2], stat_sem.at[0], plus)
-    lax.fori_loop(1, n_dp, score_wait, 0)
-
-    def add_step(d, total):
-        return total + jnp.where(row == wanted[d], scores[d], 0.0)
-
-    values[...] = lax.fori_loop(0, n_dp, add_step, node)
-    await_send(scores.at[pl.ds(0, n_dp - 1)], send_sem.at[3], score_sem.at[0], plus)
+    own = jnp.broadcast_to(jnp.sum(node, axis=0, keepdims=True), node.shape)
+    tallies[0] = jnp.where(place == me, own, 0.0)
+
+    def tally(level, sems, devices):
+        for sem, device in zip(sems, devices):
+            start_copy(
+                tallies.at[level], tally_in.at[sem], tally_send.at[sem], tally_sem.at[sem],
+                (device, mp),
+            )
+        total = tallies[level]
+        for sem, device in zip(sems, devices):
+            await_recv(tally_in.at[sem], tally_send.at[sem], tally_sem.at[sem], (device, mp))
+            total = total + tally_in[sem]
+        tallies[level + 1] = total
+
+    tally(0, (0,), (g_kv.sibling,))
+    tally(1, (1, 2, 3), [g_kv.device(step, 0) for step in (1, 2, 3)])
+    tally(2, (4, 5, 6), [g_kv.device(0, step) for step in (1, 2, 3)])
+    below = jnp.sum(hits[...] * tallies[3], axis=1, keepdims=True)
+    values[...] = node + below
+    await_send(attn.at[:, pl.ds(0, n_mp - 1)], send_sem.at[0], attn_sem.at[0], plus)
+    await_send(stats.at[pl.ds(0, n_mp - 1)], send_sem.at[1], stat_sem.at[0], plus)
+    for sem in range(7):
+        await_send(tallies.at[0], tally_send.at[sem], tally_sem.at[sem], plus)
 
 
 def on_device(hidden, norm_gain, w_query, w_kv, w_out, w_head, parents, lengths):
@@ -529,8 +593,14 @@
             pltpu.VMEM((1, width), F32),
             pltpu.VMEM((slots, heads * blk, HS), BF16),
             pltpu.VMEM((slots, blk, 2 * HS), BF16),
-            pltpu.VMEM((n_dp, blk, 2 * HS), BF16),
-            pltpu.VMEM((n_dp, blk, 2 * HS), BF16),
+            pltpu.VMEM((4, 4, blk, 2 * HS), BF16),
+            pltpu.VMEM((4, 4, blk, 2 * HS), BF16),
+            pltpu.VMEM((3, 4, blk, 2 * HS), BF16),
+            pltpu.VMEM((3, 4, blk, 2 * HS), BF16),
+            pltpu.VMEM((4, blk, 2 * HS), BF16),
+            pltpu.VMEM((3, blk, 2 * HS), BF16),
+            pltpu.VMEM((3, blk, 2 * HS), BF16),
+            pltpu.VMEM((4, 4, 2, blk, 2 * HS), BF16),
             pltpu.VMEM((far, HS), BF16),
             pltpu.VMEM((far, 2 * HS), BF16),
             pltpu.VMEM((slots, blk, 2 * HS), BF16),
@@ -540,8 +610,9 @@
             pltpu.VMEM((slots, blk, share), F32),
             pltpu.VMEM((16, 128), F32),
             pltpu.VMEM((n_mp, 16, 128), F32),
-            pltpu.VMEM((n_dp, 8, 128), F32),
-            pltpu.SMEM((n_dp,), jnp.int32),
+            pltpu.VMEM((4, 8, 128), F32),
+            pltpu.VMEM((7, 8, 128), F32),
+            pltpu.VMEM((8, 128), F32),
             dma((4 + slots,)),
             dma((10,)),
             dma((10,)),
@@ -549,12 +620,16 @@
             dma((10,)),
             dma((10,)),
             dma((10,)),
+            dma((10,)),
+            dma((10,)),
             dma((2,)),
-            dma((4,)),
-            dma((n_dp,)),
+            dma((10,)),
+            dma((10,)),
+            dma((2,)),
             dma((slots * n_mp,)),
             dma((n_mp,)),
-            dma((n_dp,)),
+            dma((7,)),
+            dma((7,)),
         ],
         compiler_params=pltpu.CompilerParams(
             collective_id=0, has_side_effects=True, vmem_limit_bytes=60 * 1024 * 1024

time: 159 us -> 161 us (1.013)
  no operation moved by 1% of the time
where the time goes in v3:
time: 161 us; the launch traced here: 159 us
  Pallas kernels  155 us (96%)
  local copies, waits for them, and re-layouts  3.4 us (2%)
    pallas_call x1, Pallas kernels, on_device(): pl.pallas_call(functools.partial(kernel, n_dp, n_mp, slots, levels), out_...  155 us

profile of v3, /device:TPU:1, one launch (start us, length us, event | category | flops | bytes accessed | tf_op | source)
XLA Modules:
  0.0 159.5 jit_solution(4888923720909512806)
XLA Ops:
  0.6 155.4 %shard_map.95 = (bf16[768,512]{1,0:T(8,128)(2,1)}, f32[8,128]{1,0:T(8,128)}) custom-call(bf16[6,128,4096]{2,1,0:T(8,128)(2,1)} %hidden.1, bf16[32,128]{1,0:T(8,128)(2,1)} %bitcast.7, bf16[128,512]{1,0:T(8,128)(2,1)} %w_query.1, bf16[128,2,128]{2,1,0:T(2,128)(2,1)} %w_kv.1, bf16[512,128]{1,0:T(8,128)(2,1)} %w_out.1, f32[32,128]{1,0:T(8,128)} %bitcast.5, ...), custom_call_target="tpu_custom_call" | custom-call | tf_op jit(solution)/shard_map/pallas_call | solution.py:578
  156.1 1.3 slice_reduce_fusion
  157.4 2.1 %copy.11 = bf16[6,128,512]{2,1,0:T(8,128)(2,1)} copy(bf16[6,128,512]{2,1,0:T(8,128)(2,1)} %bitcast.4) | data formatting | bytes 1572864

commit v4 on v3

--- a/solution.py
+++ b/solution.py
@@ -118,9 +118,9 @@
     out, values,
     x, own_hidden, wq, wkv, wo, kv_own, gains, q, kv, pair_out, pair_in, ring_out, ring_in, column_own,
     col_out, col_in, table, keys, vals, near_v, near_w, far_w,
-    attn, partial, stat, stats, tallies, tally_in, hits,
-    local_sem, kv_send, q_send, o_send, t_send, kv_sem, q_sem, o_sem, t_sem, sort_sem,
-    route_send, route_sem, send_sem, attn_sem, stat_sem, tally_send, tally_sem,
+    attn, far_out, far_in, partial, stat, stats, tallies, tally_in, hits,
+    local_sem, kv_send, q_send, far_send, own_send, t_send, kv_sem, q_sem, far_sem, own_sem, t_sem, sort_send,
+    sort_sem, route_send, route_sem, send_sem, attn_sem, cross_sem, stat_sem, tally_send, tally_sem,
 ):
     me = lax.axis_index("dp")
     mp = lax.axis_index("mp")
@@ -137,9 +137,45 @@
     def mp_at(step):
         return lax.rem(mp + step, n_mp)
 
-    sort_to = (lax.rem(me, 4) * 8 + mp, lax.div(me, 4))
-    sort_from = (mp * 4 + lax.div(me, 8), lax.rem(me, 8))
-    stays = (sort_to[0] == me) & (sort_to[1] == mp)
+    def place_of(plane, cut):
+        i = lax.rem(plane + n_mp - 2 * cut, n_mp)
+        return lax.div(i, 4), lax.rem(i, 4)
+
+    def plane_at(cut, side, j):
+        return lax.rem(2 * cut + side * 4 + j, n_mp)
+
+    halves = [place_of(mp, cut) for cut in range(2)]
+    end_cut = jnp.where((halves[0][1] == 0) | (halves[0][1] == 3), 0, 1)
+    end_half, end_j = place_of(mp, end_cut)
+    outward = jnp.where(end_j == 3, 1, n_mp - 1)
+
+    def sort_target(cut):
+        columns = lax.div(me, 4)
+        their_half, their_j = place_of(columns, cut)
+        half, j = place_of(mp, cut)
+        same = their_half == half
+        across = jnp.where(their_j < 2, their_j, 3 - their_j)
+        end = plane_at(cut, half, jnp.where(their_j < 2, 3, 0))
+        block = jnp.where(same, cut, across) * 16 + j * 4 + lax.rem(me, 4)
+        return (block, jnp.where(same, columns, end)), jnp.where(same, 0, 1)
+
+    def sort_source(kind):
+        which, j, column = lax.div(me, 16), lax.div(lax.rem(me, 16), 4), lax.rem(me, 4)
+        if kind == 0:
+            half = jnp.where(which == 0, halves[0][0], halves[1][0])
+            return mp * 4 + column, plane_at(which, half, j)
+        columns = lax.rem(mp + outward * (which + 1), n_mp)
+        return columns * 4 + column, plane_at(end_cut, end_half, j)
+
+    def is_me(device):
+        return (device[0] == me) & (device[1] == mp)
+
+    sort_to = [sort_target(cut) for cut in range(2)]
+    sort_from = [sort_source(kind) for kind in range(2)]
+    strangers = [device for device, _ in sort_to] + sort_from
+
+    def wo_block(kind, block):
+        return wo.at[kind, lax.div(block, 8), lax.div(lax.rem(block, 8), 2), lax.rem(block, 2)]
 
     kv_copy = pltpu.make_async_copy(w_kv, kv_own, local_sem.at[0])
     q_copy = pltpu.make_async_copy(w_query, wq.at[chip_y, chip_x, core], local_sem.at[1])
@@ -168,7 +204,8 @@
 
     g_kv = Gather(wkv, kv_send, kv_sem, me, mp)
     g_q = Gather(wq, q_send, q_sem, me, mp)
-    g_o = Gather(wo, o_send, o_sem, me, mp)
+    g_far = Gather(wo.at[1], far_send, far_sem, me, mp)
+    g_own = Gather(wo.at[0], own_send, own_sem, me, mp)
     g_t = Gather(table, t_send, t_sem, me, mp)
     for step in (1, 3, 2):
         greet((g_kv.device(step, 0), mp))
@@ -176,10 +213,10 @@
     greet((g_kv.sibling, mp))
     lax.fori_loop(1, n_mp, greet_mp, 0)
 
-    @pl.when(jnp.logical_not(stays))
-    def _():
-        greet(sort_to)
-        greet(sort_from)
+    for stranger in strangers:
+        @pl.when(jnp.logical_not(is_me(stranger)))
+        def _():
+            greet(stranger)
 
     for i in range(width // HS):
         gains[:, i * HS : (i + 1) * HS] = gain[i : i + 1, :].astype(F32)
@@ -203,19 +240,20 @@
     norm_segment(0)
     norm_segment(1)
     peers = 7 + n_mp - 1
-    pl.semaphore_wait(barrier, jnp.where(stays, peers, peers + 2))
+    for stranger in strangers:
+        peers = peers + jnp.where(is_me(stranger), 0, 1)
+    pl.semaphore_wait(barrier, peers)
 
     g_kv.begin()
+    q_copy.wait()
+    g_q.begin()
     norm_segment(2)
     norm_segment(3)
     g_kv.first_done()
-    q_copy.wait()
-    g_q.begin()
     norm_segment(4)
     norm_segment(5)
-
+    g_q.first_done()
     g_kv.second_done()
-    g_q.first_done()
     g_kv.all_done()
 
     group = slots // 2
@@ -303,21 +341,26 @@
 
     plus, minus = (me, mp_at(1)), (me, mp_at(n_mp - 1))
 
-    sort_slot = wo.at[lax.rem(me, 4), lax.div(mp, 2), lax.rem(mp, 2)]
-    local_sort = pltpu.make_async_copy(w_out, sort_slot, local_sem.at[2])
-
-    @pl.when(stays)
-    def _():
-        local_sort.start()
-
-    @pl.when(jnp.logical_not(stays))
-    def _():
-        start_copy(w_out, sort_slot, sort_sem.at[0], sort_sem.at[1], sort_to)
-
     route_ring()
+    route_column()
     g_q.second_done()
-    route_column()
+    g_t.first_done()
     g_q.all_done()
+
+    sort_local = [
+        pltpu.make_async_copy(w_out, wo_block(kind, device[0]), local_sem.at[4 + slots + cut])
+        for cut, (device, kind) in enumerate(sort_to)
+    ]
+    for cut, (device, kind) in enumerate(sort_to):
+        @pl.when(is_me(device))
+        def _():
+            sort_local[cut].start()
+
+        @pl.when(jnp.logical_not(is_me(device)))
+        def _():
+            start_copy(
+                w_out, wo_block(kind, device[0]), sort_send.at[cut], sort_sem.at[kind], device
+            )
 
     q_scale = math.log2(math.e) / HS**0.5
 
@@ -331,9 +374,7 @@
                 q[i * group + r, h * blk : (h + 1) * blk, :] = piece.astype(BF16)
         return carry
 
-    lax.fori_loop(0, 1, q_step, 0)
-    g_t.first_done()
-    lax.fori_loop(1, slots // group, q_step, 0)
+    lax.fori_loop(0, slots // group, q_step, 0)
 
     token = lax.broadcasted_iota(jnp.int32, (blk, HS), 0)
 
@@ -366,16 +407,17 @@
     g_t.second_done()
     g_t.all_done()
 
-    @pl.when(stays)
-    def _():
-        local_sort.wait()
-
-    @pl.when(jnp.logical_not(stays))
-    def _():
-        own_slot = wo.at[chip_y, chip_x, core]
-        await_recv(own_slot, sort_sem.at[0], sort_sem.at[1], sort_from)
-
-    g_o.begin()
+    for cut, (device, _) in enumerate(sort_to):
+        @pl.when(is_me(device))
+        def _():
+            sort_local[cut].wait()
+
+    for kind in range(2):
+        @pl.when(jnp.logical_not(is_me(sort_from[kind])))
+        def _():
+            await_recv(wo_block(kind, me), sort_send.at[0], sort_sem.at[kind], sort_from[kind])
+
+    g_far.begin()
 
     def far_step(j, carry):
         node = parents[j, first_node]
@@ -394,9 +436,6 @@
     lax.fori_loop(0, levels, far_step, 0)
 
     chunk = 512
-    sides = ((0, plus, n_mp - 1), (1, minus, 1))
-    half = blk // 2
-
     def attend(s):
         def score_step(j, carry):
             cols = pl.ds(pl.multiple_of(j * chunk, chunk), chunk)
@@ -413,43 +452,104 @@
         for h in range(heads):
             attn[s, mp, :, h * HS : (h + 1) * HS] = mean[h * blk : (h + 1) * blk].astype(BF16)
 
-    def attn_part(s, side, hop):
-        source = mp_at((n_mp - hop) if side == 0 else hop)
-        if hop == n_mp // 2:
-            return attn.at[s, source, pl.ds(side * half, half), :]
-        return attn.at[s, source]
+    third = slots // 2
 
     def attn_sem_at(s, side, hop):
-        return attn_sem.at[(s * 2 + side) * (n_mp // 2) + hop - 1]
-
-    def send_on(s, hop):
-        for side, device, _ in sides:
-            if hop > 0:
-                ref = attn_part(s, side, hop)
-                await_recv(ref, send_sem.at[0], attn_sem_at(s, side, hop), device)
-            source = mp_at((n_mp - hop) if side == 0 else hop)
-            ref = attn.at[s, source]
-            if hop + 1 == n_mp // 2:
-                ref = attn.at[s, source, pl.ds(side * half, half), :]
-            start_copy(ref, ref, send_sem.at[0], attn_sem_at(s, side, hop + 1), device)
-
-    def attend_step(s, carry):
+        return attn_sem.at[(s * 2 + side) * 3 + hop - 1]
+
+    def attn_send(s, source, side, hop):
+        ref = attn.at[s, source]
+        start_copy(ref, ref, send_sem.at[0], attn_sem_at(s, side, hop), (plus, minus)[side])
+
+    def relay(s, hop):
+        j = halves[s // third][1]
+        for side, left, more in ((0, j, j < 3), (1, 3 - j, j > 0)):
+            source = mp_at(n_mp - hop if side == 0 else hop)
+
+            @pl.when(left >= hop)
+            def _():
+                ref = attn.at[s, source]
+                await_recv(ref, send_sem.at[0], attn_sem_at(s, side, hop), plus)
+
+            if hop < 3:
+                @pl.when((left >= hop) & more)
+                def _():
+                    attn_send(s, source, side, hop + 1)
+
+    def attend_step(n, carry):
+        cut = lax.rem(n, 2)
+        s = cut * third + lax.div(n, 2)
         attend(s)
-        send_on(s, 0)
-
-        @pl.when(s == 1)
-        def _():
-            g_o.first_done()
+        _, j = place_of(mp, cut)
+
+        @pl.when(j < 3)
+        def _():
+            attn_send(s, mp, 0, 1)
+
+        @pl.when(j > 0)
+        def _():
+            attn_send(s, mp, 1, 1)
+
+        @pl.when(n == 1)
+        def _():
+            g_far.first_done()
+            g_own.begin()
 
         return carry
 
     lax.fori_loop(0, slots, attend_step, 0)
-    for s in range(slots):
-        send_on(s, 1)
-    g_o.second_done()
-    for s in range(slots):
-        send_on(s, 2)
-    g_o.all_done()
+
+    def relays(u, hop):
+        relay(u, hop)
+        relay(third + u, hop)
+
+    def product(s, cut, half, kind, first):
+        rows = jnp.concatenate([attn[s, plane_at(cut, half, k)] for k in range(4)], axis=1)
+        parts = []
+        for pair in range(2):
+            cols = []
+            for r in (2 * pair, 2 * pair + 1):
+                blocks = []
+                for k in range(4):
+                    t = k * 4 + r
+                    blocks.append(wo[kind, first + t // 8, t % 8 // 2, t % 2])
+                cols.append(jnp.concatenate(blocks, axis=0))
+            weight = jnp.concatenate(cols, axis=1)
+            parts.append(jnp.dot(rows, weight, preferred_element_type=F32))
+        return jnp.concatenate(parts, axis=1)
+
+    def across(u):
+        s = end_cut * third + u
+        for n in range(2):
+            far_out[u, n] = product(s, end_cut, end_half, 1, 2 * n).astype(BF16)
+            to = lax.rem(mp + outward * (n + 1), n_mp)
+            start_copy(far_out.at[u, n], far_in.at[s], send_sem.at[2], cross_sem.at[s], (me, to))
+
+    relays(0, 1)
+    relays(1, 1)
+    g_own.first_done()
+    relays(0, 2)
+    g_far.second_done()
+    relays(2, 1)
+    relays(1, 2)
+    relays(0, 3)
+    g_far.all_done()
+    across(0)
+    relays(2, 2)
+    relays(1, 3)
+    across(1)
+    relays(2, 3)
+    across(2)
+    g_own.second_done()
+    g_own.all_done()
+
+    def own_step(u, carry):
+        for cut in range(2):
+            s = cut * third + u
+            partial[s] = product(s, cut, halves[cut][0], 0, 2 * cut)
+        return carry
+
+    lax.fori_loop(0, third, own_step, 0)
 
     row = lax.broadcasted_iota(jnp.int32, (8, 128), 0)
     place = lax.broadcasted_iota(jnp.int32, (8, 128), 1)
@@ -464,42 +564,18 @@
     hits[...] = lax.fori_loop(0, n_dp, hit_step, jnp.zeros((8, 128), F32))
 
     g_q.end()
-    g_o.end()
+    g_far.end()
+    g_own.end()
     g_t.end()
     route_end()
-
-    @pl.when(jnp.logical_not(stays))
-    def _():
-        await_send(wo.at[chip_y, chip_x, core], sort_sem.at[0], sort_sem.at[1], sort_to)
-
-    def weight_at(sources, pair):
-        cols = []
-        for j in (2 * pair, 2 * pair + 1):
-            rows = [wo[j, lax.div(m, 2), lax.rem(m, 2)] for m in sources]
-            cols.append(jnp.concatenate(rows, axis=0) if len(rows) > 1 else rows[0])
-        return jnp.concatenate(cols, axis=1)
-
-    opposite = mp_at(n_mp // 2)
-    others = [mp_at(i) for i in range(n_mp) if i != n_mp // 2]
-
-    def most(s, carry):
-        send_on(s, 3)
-        rows = jnp.concatenate([attn[s, m] for m in others], axis=1)
-        for pair in range(2):
-            cols = slice(pair * 2 * HS, (pair + 1) * 2 * HS)
-            partial[s, :, cols] = jnp.dot(
-                rows, weight_at(others, pair), preferred_element_type=F32
-            )
-        return carry
-
-    lax.fori_loop(0, slots, most, 0)
+    for cut, (device, kind) in enumerate(sort_to):
+        @pl.when(jnp.logical_not(is_me(device)))
+        def _():
+            await_send(w_out, sort_send.at[cut], sort_sem.at[0], device)
 
     def finish(s, carry):
-        for side, device, _ in sides:
-            ref = attn_part(s, side, n_mp // 2)
-            await_recv(ref, send_sem.at[0], attn_sem_at(s, side, n_mp // 2), device)
-        weight = jnp.concatenate([weight_at([opposite], pair) for pair in range(2)], axis=1)
-        total = partial[s] + jnp.dot(attn[s, opposite], weight, preferred_element_type=F32)
+        await_recv(far_in.at[s], send_sem.at[2], cross_sem.at[s], plus)
+        total = partial[s] + far_in[s].astype(F32)
         result = (own_hidden[s].astype(F32) + total).astype(BF16)
         out[pl.ds(pl.multiple_of(s * blk, blk), blk), :] = result
         floats = result.astype(F32)
@@ -557,7 +633,8 @@
     tally(2, (4, 5, 6), [g_kv.device(0, step) for step in (1, 2, 3)])
     below = jnp.sum(hits[...] * tallies[3], axis=1, keepdims=True)
     values[...] = node + below
-    await_send(attn.at[:, pl.ds(0, n_mp - 1)], send_sem.at[0], attn_sem.at[0], plus)
+    await_send(attn.at[:, pl.ds(0, 3)], send_sem.at[0], attn_sem.at[0], plus)
+    await_send(far_out, send_sem.at[2], cross_sem.at[0], plus)
     await_send(stats.at[pl.ds(0, n_mp - 1)], send_sem.at[1], stat_sem.at[0], plus)
     for sem in range(7):
         await_send(tallies.at[0], tally_send.at[sem], tally_sem.at[sem], plus)
@@ -588,7 +665,7 @@
             pltpu.VMEM((slots, blk, share), BF16),
             pltpu.VMEM((4, 4, 2, depth, q_columns), BF16),
             pltpu.VMEM((4, 4, 2, depth, 2 * HS), BF16),
-            pltpu.VMEM((4, 4, 2) + w_out.shape, BF16),
+            pltpu.VMEM((2, 4, 4, 2) + w_out.shape, BF16),
             pltpu.VMEM(w_kv.shape, BF16),
             pltpu.VMEM((1, width), F32),
             pltpu.VMEM((slots, heads * blk, HS), BF16),
@@ -607,13 +684,17 @@
             pltpu.VMEM((slots, heads * blk, blk), BF16),
             pltpu.VMEM((heads * blk, far), BF16),
             pltpu.VMEM((slots, n_mp, blk, q_columns), BF16),
+            pltpu.VMEM((slots // 2, 2, blk, share), BF16),
+            pltpu.VMEM((slots, blk, share), BF16),
             pltpu.VMEM((slots, blk, share), F32),
             pltpu.VMEM((16, 128), F32),
             pltpu.VMEM((n_mp, 16, 128), F32),
             pltpu.VMEM((4, 8, 128), F32),
             pltpu.VMEM((7, 8, 128), F32),
             pltpu.VMEM((8, 128), F32),
-            dma((4 + slots,)),
+            dma((6 + slots,)),
+            dma((10,)),
+            dma((10,)),
             dma((10,)),
             dma((10,)),
             dma((10,)),
@@ -623,10 +704,12 @@
             dma((10,)),
             dma((10,)),
             dma((2,)),
-            dma((10,)),
-            dma((10,)),
             dma((2,)),
-            dma((slots * n_mp,)),
+            dma((10,)),
+            dma((10,)),
+            dma((3,)),
+            dma((slots * 6,)),
+            dma((slots,)),
             dma((n_mp,)),
             dma((7,)),
             dma((7,)),

time: 161 us -> 147 us (0.913)
  Pallas kernels: 155 us -> 143 us
    pallas_call x1, Pallas kernels: 155 us -> 143 us  [on_device(): pl.pallas_call(functools.partial(kernel, n_dp, n_mp, slots, levels), out_...]
where the time goes in v4:
time: 147 us
  Pallas kernels  143 us (97%)
  local copies, waits for them, and re-layouts  3.4 us (2%)
    pallas_call x1, Pallas kernels, on_device(): pl.pallas_call(functools.partial(kernel, n_dp, n_mp, slots, levels), out_...  143 us

profile of v4, /device:TPU:1, one launch (start us, length us, event | category | flops | bytes accessed | tf_op | source)
XLA Modules:
  0.0 146.7 jit_solution(2527644158249518692)
XLA Ops:
  0.6 142.7 %shard_map.95 = (bf16[768,512]{1,0:T(8,128)(2,1)}, f32[8,128]{1,0:T(8,128)}) custom-call(bf16[6,128,4096]{2,1,0:T(8,128)(2,1)} %hidden.1, bf16[32,128]{1,0:T(8,128)(2,1)} %bitcast.7, bf16[128,512]{1,0:T(8,128)(2,1)} %w_query.1, bf16[128,2,128]{2,1,0:T(2,128)(2,1)} %w_kv.1, bf16[512,128]{1,0:T(8,128)(2,1)} %w_out.1, f32[32,128]{1,0:T(8,128)} %bitcast.5, ...), custom_call_target="tpu_custom_call" | custom-call | tf_op jit(solution)/shard_map/pallas_call | solution.py:655
  143.3 1.3 slice_reduce_fusion
  144.6 2.1 %copy.11 = bf16[6,128,512]{2,1,0:T(8,128)(2,1)} copy(bf16[6,128,512]{2,1,0:T(8,128)(2,1)} %bitcast.4) | data formatting | bytes 1572864

commit v5 on v4

--- a/solution.py
+++ b/solution.py
@@ -119,7 +119,7 @@
     x, own_hidden, wq, wkv, wo, kv_own, gains, q, kv, pair_out, pair_in, ring_out, ring_in, column_own,
     col_out, col_in, table, keys, vals, near_v, near_w, far_w,
     attn, far_out, far_in, partial, stat, stats, tallies, tally_in, hits,
-    local_sem, kv_send, q_send, far_send, own_send, t_send, kv_sem, q_sem, far_sem, own_sem, t_sem, sort_send,
+    local_sem, kv_send, q_send, far_send, own_send, t_send, kv_sem, q_sem, far_sem, own_sem, t_sem, out_sem, sort_send,
     sort_sem, route_send, route_sem, send_sem, attn_sem, cross_sem, stat_sem, tally_send, tally_sem,
 ):
     me = lax.axis_index("dp")
@@ -127,7 +127,7 @@
     width = x.shape[1]
     blk = x.shape[0] // slots
     heads = wq.shape[-1] // HS
-    share = out.shape[1]
+    share = out.shape[2]
     far = levels * blk
     core = lax.rem(me, 2)
     chip_x = lax.rem(lax.div(me, 2), 4)
@@ -207,10 +207,14 @@
     g_far = Gather(wo.at[1], far_send, far_sem, me, mp)
     g_own = Gather(wo.at[0], own_send, own_sem, me, mp)
     g_t = Gather(table, t_send, t_sem, me, mp)
-    for step in (1, 3, 2):
-        greet((g_kv.device(step, 0), mp))
-        greet((g_kv.device(0, step), mp))
-    greet((g_kv.sibling, mp))
+    def dp_near(on_x, on_y, flip):
+        chip = lax.rem(chip_y + on_y, 4) * 8 + lax.rem(chip_x + on_x, 4) * 2
+        return chip + lax.rem(core + flip, 2)
+
+    row_devices = [dp_near(i, 0, flip) for flip in (0, 1) for i in (2, 1, 3)] + [dp_near(0, 0, 1)]
+    column_devices = [dp_near(0, i, 0) for i in (2, 1, 3)]
+    for device in row_devices + column_devices:
+        greet((device, mp))
     lax.fori_loop(1, n_mp, greet_mp, 0)
 
     for stranger in strangers:
@@ -239,7 +243,7 @@
     wkv[chip_y, chip_x, core, :, HS:] = kv_own[:, 1, :]
     norm_segment(0)
     norm_segment(1)
-    peers = 7 + n_mp - 1
+    peers = 10 + n_mp - 1
     for stranger in strangers:
         peers = peers + jnp.where(is_me(stranger), 0, 1)
     pl.semaphore_wait(barrier, peers)
@@ -526,17 +530,17 @@
             start_copy(far_out.at[u, n], far_in.at[s], send_sem.at[2], cross_sem.at[s], (me, to))
 
     relays(0, 1)
-    relays(1, 1)
     g_own.first_done()
     relays(0, 2)
+    relays(1, 1)
+    relays(0, 3)
+    relays(1, 2)
+    relays(2, 1)
     g_far.second_done()
-    relays(2, 1)
-    relays(1, 2)
-    relays(0, 3)
     g_far.all_done()
     across(0)
+    relays(1, 3)
     relays(2, 2)
-    relays(1, 3)
     across(1)
     relays(2, 3)
     across(2)
@@ -573,11 +577,16 @@
         def _():
             await_send(w_out, sort_send.at[cut], sort_sem.at[0], device)
 
-    def finish(s, carry):
+    def out_copy(s):
+        return pltpu.make_async_copy(own_hidden.at[s], out.at[s], out_sem.at[s])
+
+    def finish(n, carry):
+        s = lax.rem(n, 2) * third + lax.div(n, 2)
         await_recv(far_in.at[s], send_sem.at[2], cross_sem.at[s], plus)
         total = partial[s] + far_in[s].astype(F32)
         result = (own_hidden[s].astype(F32) + total).astype(BF16)
-        out[pl.ds(pl.multiple_of(s * blk, blk), blk), :] = result
+        own_hidden[s] = result
+        out_copy(s).start()
         floats = result.astype(F32)
         heads_at = mp * (share // HS)
         head = jnp.concatenate(
@@ -628,15 +637,16 @@
             total = total + tally_in[sem]
         tallies[level + 1] = total
 
-    tally(0, (0,), (g_kv.sibling,))
-    tally(1, (1, 2, 3), [g_kv.device(step, 0) for step in (1, 2, 3)])
-    tally(2, (4, 5, 6), [g_kv.device(0, step) for step in (1, 2, 3)])
-    below = jnp.sum(hits[...] * tallies[3], axis=1, keepdims=True)
+    tally(0, range(7), row_devices)
+    tally(1, range(7, 10), column_devices)
+    below = jnp.sum(hits[...] * tallies[2], axis=1, keepdims=True)
     values[...] = node + below
     await_send(attn.at[:, pl.ds(0, 3)], send_sem.at[0], attn_sem.at[0], plus)
     await_send(far_out, send_sem.at[2], cross_sem.at[0], plus)
     await_send(stats.at[pl.ds(0, n_mp - 1)], send_sem.at[1], stat_sem.at[0], plus)
-    for sem in range(7):
+    for s in range(slots):
+        out_copy(s).wait()
+    for sem in range(10):
         await_send(tallies.at[0], tally_send.at[sem], tally_sem.at[sem], plus)
 
 
@@ -655,11 +665,11 @@
     layer, values = pl.pallas_call(
         functools.partial(kernel, n_dp, n_mp, slots, levels),
         out_shape=(
-            jax.ShapeDtypeStruct((slots * blk, share), BF16),
+            jax.ShapeDtypeStruct((slots, blk, share), BF16),
             jax.ShapeDtypeStruct((8, 128), F32),
         ),
         in_specs=[any_space, vmem, any_space, any_space, any_space, vmem, smem, smem],
-        out_specs=(vmem, vmem),
+        out_specs=(any_space, vmem),
         scratch_shapes=[
             pltpu.VMEM((slots * blk, width), BF16),
             pltpu.VMEM((slots, blk, share), BF16),
@@ -689,8 +699,8 @@
             pltpu.VMEM((slots, blk, share), F32),
             pltpu.VMEM((16, 128), F32),
             pltpu.VMEM((n_mp, 16, 128), F32),
-            pltpu.VMEM((4, 8, 128), F32),
-            pltpu.VMEM((7, 8, 128), F32),
+            pltpu.VMEM((3, 8, 128), F32),
+            pltpu.VMEM((10, 8, 128), F32),
             pltpu.VMEM((8, 128), F32),
             dma((6 + slots,)),
             dma((10,)),
@@ -703,6 +713,7 @@
             dma((10,)),
             dma((10,)),
             dma((10,)),
+            dma((slots,)),
             dma((2,)),
             dma((2,)),
             dma((10,)),
@@ -711,8 +722,8 @@
             dma((slots * 6,)),
             dma((slots,)),
             dma((n_mp,)),
-            dma((7,)),
-            dma((7,)),
+            dma((10,)),
+            dma((10,)),
         ],
         compiler_params=pltpu.CompilerParams(
             collective_id=0, has_side_effects=True, vmem_limit_bytes=60 * 1024 * 1024
@@ -721,7 +732,7 @@
         hidden, norm_gain.reshape(width // HS, HS), w_query, w_kv, w_out,
         w_head.reshape(width // HS, HS), parents.T, lengths,
     )
-    return layer.reshape(slots, blk, share), values[:slots, 0]
+    return layer, values[:slots, 0]
 
 
 def solution(mesh):

time: 147 us -> 144 us (0.980)
  Pallas kernels: 143 us -> 140 us
    pallas_call x1, Pallas kernels: 143 us -> 140 us  [on_device(): pl.pallas_call(functools.partial(kernel, n_dp, n_mp, slots, levels), out_...]
where the time goes in v5:
time: 144 us
  Pallas kernels  140 us (97%)
  local copies, waits for them, and re-layouts  3.4 us (2%)
    pallas_call x1, Pallas kernels, on_device(): pl.pallas_call(functools.partial(kernel, n_dp, n_mp, slots, levels), out_...  140 us

profile of v5, /device:TPU:1, one launch (start us, length us, event | category | flops | bytes accessed | tf_op | source)
XLA Modules:
  0.0 143.8 jit_solution(4033044148927027607)
XLA Ops:
  0.6 139.8 %shard_map.95 = (bf16[6,128,512]{2,1,0:T(8,128)(2,1)}, f32[8,128]{1,0:T(8,128)}) custom-call(bf16[6,128,4096]{2,1,0:T(8,128)(2,1)} %hidden.1, bf16[32,128]{1,0:T(8,128)(2,1)} %bitcast.5, bf16[128,512]{1,0:T(8,128)(2,1)} %w_query.1, bf16[128,2,128]{2,1,0:T(2,128)(2,1)} %w_kv.1, bf16[512,128]{1,0:T(8,128)(2,1)} %w_out.1, f32[32,128]{1,0:T(8,128)} %bitcast.3, ...), custom_call_target="tpu_custom_call" | custom-call | tf_op jit(solution)/shard_map/pallas_call | solution.py:665
  140.4 1.3 slice_reduce_fusion
  141.7 2.1 %copy.11 = bf16[6,128,512]{2,1,0:T(8,128)(2,1)} copy(bf16[6,128,512]{2,1,0:T(8,128)(2,1)} %get-tuple-element.8) | data formatting | bytes 1572864
